TPU v7x, 32 devices: a whole 2x2x4 slice. The times are simulated.
32 devices in a mesh: groups: 2 (over x), seq: 8 (over z, y), tensor: 2 (over core).
Axes of the slice: x: 2, y: 2, z: 4, core: 2. Of those that a mesh axis runs over, the one named last changes fastest.
Arguments:
- queries: bfloat16 [128, 2, 8192], P(('groups', 'seq'), None, 'tensor'), parts along dimension 0, may hold values from -384 to 384
- fresh_keys: bfloat16 [128, 2, 1024], P(('groups', 'seq'), None, 'tensor'), parts along dimension 0, may hold values from -24 to 24
- fresh_values: bfloat16 [128, 2, 1024], P(('groups', 'seq'), None, 'tensor'), parts along dimension 0, may hold values from -6 to 6
- residual_in: bfloat16 [128, 2, 8192], P(('groups', 'seq'), None, 'tensor'), parts along dimension 0, may hold values from -0.29882812 to 0.29882812
- cache_keys: bfloat16 [8, 8192, 128], P('tensor', ('groups', 'seq')), parts along dimension 1, may hold values from -8 to 8
- cache_values: bfloat16 [8, 8192, 128], P('tensor', ('groups', 'seq')), parts along dimension 1, may hold values from -6 to 6
- key_scales: float32 [8, 128], P('tensor', ('groups', 'seq')), parts along dimension 1, may hold values from 0.5 to 2
- value_scales: float32 [8, 128], P('tensor', ('groups', 'seq')), parts along dimension 1, may hold values from 0.5 to 2
- page_table: int32 [16, 8], P(('groups', 'seq')), parts along dimension 0, may hold values from 0 to 7, each once within a row
- row_lengths: int32 [128], P('groups'), parts along dimension 0, may hold values from 512 to 4096
- norm_gain: float32 [8192], P('tensor'), may hold values from 0.1 to 1.9
- w_gate: bfloat16 [8192, 14336], P('tensor', 'seq'), may hold values from -0.0625 to 0.0625
- w_up: bfloat16 [8192, 14336], P('tensor', 'seq'), may hold values from -0.0625 to 0.0625
- w_down: bfloat16 [14336, 8192], P('seq', 'tensor'), may hold values from -0.046875 to 0.046875
Outputs:
- layer_out: bfloat16 [128, 2, 8192], P(('groups', 'seq'), None, 'tensor'), parts along dimension 0
There are 2 independent parts, one for each index of `groups`. A program takes and returns all parts, laid end to end along the dimension named above; an argument that names none is the same for every part. Nothing has to cross between parts.
Inputs may be any that keep to these rules, and one draw needn't show every extreme that they name: Each row of page_table names each of its seq index's pages once. `row_lengths`: every row sees at least the cache positions of the first seq index.
All inputs are finite; a program needn't handle non-finite values.
Results may differ from a plain program's by a relative error of at most 0.0064.
Values may be sent and summed in bfloat16 or wider, within the bound.
A program may use at most 128 MiB of HBM per device.

v0:
```python
import math

import jax
import jax.numpy as jnp
from jax import lax
from jax.sharding import PartitionSpec as P

D = 8192


NEG_FILL = -1e30
EPSILON = 1e-05
LOG2E = 1.4426950408889634


def combine_partials(earlier, later):
    shared_top = jnp.maximum(earlier[0], later[0])
    early_factor = jnp.exp2(earlier[0] - shared_top)
    late_factor = jnp.exp2(later[0] - shared_top)
    return (
        shared_top,
        earlier[1] * early_factor + later[1] * late_factor,
        earlier[2] * early_factor[..., None] + later[2] * late_factor[..., None],
    )


def masked_terms(scores, allowed_mask):
    row_top = jnp.ceil(jnp.max(jnp.where(allowed_mask, scores, NEG_FILL), axis=-1))
    exp_terms = jnp.where(allowed_mask, jnp.exp2(scores - row_top[..., None]), 0.0)
    return (row_top, exp_terms)


def body(
    queries,
    fresh_keys,
    fresh_values,
    residual_in,
    cache_keys,
    cache_values,
    key_scales,
    value_scales,
    page_table,
    row_lengths,
    norm_gain,
    w_gate,
    w_up,
    w_down,
):
    local_rows = queries.shape[0]
    step_count = queries.shape[1]
    half_width = queries.shape[2]
    groups = cache_keys.shape[0]
    cache_span = cache_keys.shape[1]
    head_dim = cache_keys.shape[2]
    page_count = page_table.shape[1]
    block_size = cache_span // page_count
    heads_per = half_width // (groups * head_dim)
    inv_root = LOG2E / math.sqrt(head_dim)
    seq_index = lax.axis_index("seq")
    all_q, all_fk, all_fv, all_x = (
        lax.all_gather(queries, "seq", axis=0, tiled=True),
        lax.all_gather(fresh_keys, "seq", axis=0, tiled=True),
        lax.all_gather(fresh_values, "seq", axis=0, tiled=True),
        lax.all_gather(residual_in, "seq", axis=0, tiled=True),
    )
    all_rows = all_q.shape[0]
    offsets = jnp.arange(cache_span, dtype=jnp.int32)
    logical = seq_index * page_count + jnp.repeat(page_table[0], block_size)
    position = logical * block_size + offsets % block_size
    visible = position[None, :] < row_lengths[:, None]
    k_scale = jnp.repeat(key_scales, block_size, axis=1)
    v_scale = jnp.repeat(value_scales, block_size, axis=1)
    q_part = all_q.reshape(all_rows, step_count, groups, heads_per, head_dim)
    q_part = jnp.moveaxis(q_part, 2, 0)

    def per_group(operands):
        q_group, key_block, value_block, k_row, v_row = operands
        raw_scores = jnp.einsum(
            "nsqd,cd->nsqc", q_group, key_block, preferred_element_type=jnp.float32
        )
        scores = raw_scores * k_row * inv_root
        row_top, exp_terms = masked_terms(scores, visible[:, None, None, :])
        row_total = jnp.sum(exp_terms, axis=-1)
        weights = (exp_terms * v_row).astype(jnp.bfloat16)
        weighted = jnp.einsum(
            "nsqc,cd->nsqd", weights, value_block, preferred_element_type=jnp.float32
        )
        return (row_top, row_total, weighted)

    partial_value = lax.map(per_group, (q_part, cache_keys, cache_values, k_scale, v_scale))
    row_peak = lax.pmax(partial_value[0], "seq")
    factor = jnp.exp2(partial_value[0] - row_peak)
    row_total, weighted = lax.psum(
        (partial_value[1] * factor, partial_value[2] * factor[..., None]), "seq"
    )
    row_count = all_q.shape[0]
    fresh_row_count = all_q.shape[0]
    q_part = all_q.reshape(fresh_row_count, step_count, groups, heads_per, head_dim)
    k_part = all_fk.reshape(fresh_row_count, step_count, groups, head_dim)
    v_part = all_fv.reshape(fresh_row_count, step_count, groups, head_dim)
    raw_scores = jnp.einsum("nsgqd,ntgd->gnsqt", q_part, k_part, preferred_element_type=jnp.float32)
    scores = raw_scores * inv_root
    allowed = jnp.arange(step_count)[None, :] <= (0 + jnp.arange(step_count))[:, None]
    row_top, exp_terms = masked_terms(scores, allowed[None, None, :, None, :])
    fresh_row_total = jnp.sum(exp_terms, axis=-1)
    fresh_weighted = jnp.einsum(
        "gnsqt,ntgd->gnsqd",
        exp_terms.astype(jnp.bfloat16),
        v_part,
        preferred_element_type=jnp.float32,
    )
    joined = combine_partials(
        (row_peak, row_total, weighted), (row_top, fresh_row_total, fresh_weighted)
    )
    attention = joined[2] / joined[1][..., None]
    attention = jnp.moveaxis(attention, 0, 2).reshape(row_count, step_count, half_width)
    hidden_state = all_x.astype(jnp.float32) + attention
    square = lax.psum(jnp.sum(hidden_state * hidden_state, axis=-1), "tensor")
    inverse_rms = lax.rsqrt(square / D + EPSILON)
    normed = (hidden_state * inverse_rms[..., None] * norm_gain).astype(jnp.bfloat16)
    hidden_state, normed = (hidden_state, normed)
    own_state = lax.dynamic_slice_in_dim(hidden_state, seq_index * local_rows, local_rows, 0)
    flat_normed = normed.reshape(all_rows * step_count, half_width)
    gate_part = jnp.dot(flat_normed, w_gate, preferred_element_type=jnp.float32)
    up_part = jnp.dot(flat_normed, w_up, preferred_element_type=jnp.float32)
    gate_sums, up_sums = lax.psum((gate_part, up_part), "tensor")
    hidden = (jax.nn.silu(gate_sums) * up_sums).astype(jnp.bfloat16)
    down_sums = lax.psum_scatter(
        jnp.dot(hidden, w_down, preferred_element_type=jnp.float32),
        "seq",
        scatter_dimension=0,
        tiled=True,
    )
    return (own_state + down_sums.reshape(local_rows, step_count, half_width)).astype(jnp.bfloat16)


def solution(mesh):
    in_specs = (
        P(("groups", "seq"), None, "tensor"),
        P(("groups", "seq"), None, "tensor"),
        P(("groups", "seq"), None, "tensor"),
        P(("groups", "seq"), None, "tensor"),
        P("tensor", ("groups", "seq"), None),
        P("tensor", ("groups", "seq"), None),
        P("tensor", ("groups", "seq")),
        P("tensor", ("groups", "seq")),
        P(("groups", "seq"), None),
        P("groups"),
        P("tensor"),
        P("tensor", "seq"),
        P("tensor", "seq"),
        P("seq", "tensor"),
    )
    out_specs = P(("groups", "seq"), None, "tensor")
    return jax.shard_map(body, mesh=mesh, in_specs=in_specs, out_specs=out_specs, check_vma=False)
```

profile of v0, /device:TPU:0, one launch (start us, length us, event | category | flops | bytes accessed | tf_op | source)
XLA Modules:
  0.0 389.8 jit_solution(16728039884289439175)
XLA Ops:
  9.8 42.6 %all-gather.5.cloned.1.call-done = bf16[64,2,4096]{2,1,0:T(2,128)(2,1)} async-done(((bf16[8,2,4096]{2,1,0:T(2,128)(2,1)}), bf16[64,2,4096]{2,1,0:T(2,128)(2,1)}) %all-gather.5.cloned.1.call-update) | async-done | bytes 1048592 | tf_op jit(solution)/shard_map/all_gather | solution.py:61
  52.4 1.9 reshape.100
  54.3 21.1 %while.15 = (s32[]{:T(128)}, f32[4,64,2,8]{1,3,2,0:T(8,128)S(1)}, f32[4,64,2,8]{1,3,2,0:T(8,128)S(1)}, f32[4,64,2,8,128]{4,3,2,1,0:T(8,128)}, bf16[4,64,2,8,128]...) while((s32[]{:T(128)}, f32[4,64,2,8]{1,3,2,0:T(8,128)S(1)}, ...), condition=%wide.region_3.4_spmd.clone, body=%wide.region_0.3_spmd.clone.sunk | while | flops 277380096 | bytes 7569801 | solution.py:90
  54.4 1.6 select_reduce_fusion.3
  57.1 2.5 fusion.57
  59.7 1.6 select_reduce_fusion.3
  62.4 2.5 fusion.57
  65.0 1.6 select_reduce_fusion.3
  67.7 2.5 fusion.57
  70.3 1.6 select_reduce_fusion.3
  72.0 0.9 fusion.56
  72.9 2.5 fusion.57
  75.5 34.9 %pmax.7 = f32[4,64,2,8]{1,3,2,0:T(8,128)S(1)} all-reduce(f32[4,64,2,8]{1,3,2,0:T(8,128)S(1)} %get-tuple-element.60), channel_id=1, replica_groups=mesh['groups'=2,'seq'=8,'tensor'=2] {'seq'}, use_global_device_ids=true, to_apply=%region_4.5 | all-reduce | flops 4096 | bytes 32768 | tf_op jit(solution)/shard_map/pmax | solution.py:91
  110.5 3.6 broadcast_multiply_fusion
  115.8 32.0 %all_gather.14 = bf16[64,2,512]{2,1,0:T(2,128)(2,1)S(1)} all-gather(bf16[8,2,512]{2,1,0:T(2,128)(2,1)S(1)} %copy-done.2), channel_id=1, replica_groups=mesh['groups'=2,'seq'=8,'tensor'=2] {'seq'}, dimensions={0}, use_global_device_ids=true | all-gather | bytes 147456 | tf_op jit(solution)/shard_map/all_gather | solution.py:62
  147.9 30.8 %all_gather.15 = bf16[64,2,512]{2,1,0:T(2,128)(2,1)S(1)} all-gather(bf16[8,2,512]{2,1,0:T(2,128)(2,1)S(1)} %copy-done.3), channel_id=1, replica_groups=mesh['groups'=2,'seq'=8,'tensor'=2] {'seq'}, dimensions={0}, use_global_device_ids=true | all-gather | bytes 147456 | tf_op jit(solution)/shard_map/all_gather | solution.py:63
  178.8 4.8 %select_reduce_fusion.1 = (f32[4,64,2,8]{3,2,1,0:T(2,128)S(1)}, f32[4,64,2,8,2]{3,4,2,1,0:T(2,128)S(1)}) fusion(pred[2,2]{1,0:T(4,128)(4,1)S(1)} %iota_compare_fusion, bf16[64,2,4,128,1]{3,2,1,0,4:T(4,128)(2,1)S(1)} %bitcast.70, bf16[64,2,4,8,128]{4,3,2,1,0:T(8,128)(2,1)S(1)} %bitcast.65), kind=kOutput, calls=%fused_computation.41 | convolution fusion | flops 2117632 | bytes 1228804 | tf_op jit(solution)/shard_map/nsgqd,ntgd->gnsqt/dot_general | solution.py:101
  183.9 1.2 fusion.38
  185.2 34.1 %psum.36 = f32[4,64,2,8]{1,3,2,0:T(8,128)S(1)} all-reduce(f32[4,64,2,8]{1,3,2,0:T(8,128)S(1)} %get-tuple-element.172), channel_id=1, replica_groups=mesh['groups'=2,'seq'=8,'tensor'=2] {'seq'}, use_global_device_ids=true, to_apply=%region_7.8 | all-reduce | flops 4096 | bytes 32768 | tf_op jit(solution)/shard_map/psum | solution.py:93
  219.8 4.1 %divide_bitcast_fusion = f32[64,2,4,8,128]{4,3,1,0,2:T(8,128)S(1)} fusion(f32[4,64,2,8,128]{4,3,2,1,0:T(8,128)} %all-reduce.4.cloned.1.call-done, f32[4,64,2,8]{3,2,1,0:T(2,128)S(1)} %copy.91, f32[4,64,2,8]{3,2,1,0:T(2,128)S(1)} %copy.88, f32[4,64,2,8]{3,2,1,0:T(2,128)S(1)} %copy.84, bf16[64,2,4,128,1]{3,2,1,0,4:T(4,128)(2,1)S(1)} %bitcast.69, ...), kind=kOutput, calls=%fused_computation.34 | convolution fusion | flops 4227072 | bytes 4423684 | tf_op jit(solution)/shard_map/gnsqt,ntgd->gnsqd/dot_general | solution.py:106
  224.2 1.6 reshape.93
  225.8 31.5 %all-gather.3.cloned.1.call-done = bf16[64,2,4096]{2,0,1:T(8,128)(2,1)} async-done(((bf16[8,2,4096]{2,0,1:T(8,128)(2,1)}), bf16[64,2,4096]{2,0,1:T(8,128)(2,1)}) %all-gather.3.cloned.1.call-update) | async-done | bytes 1048592 | tf_op jit(solution)/shard_map/all_gather | solution.py:64
  257.4 2.2 multiply_reduce_fusion
  259.6 2.6 psum.37
  262.5 2.1 copy.93
  264.6 1.5 reshape.94
  266.1 8.2 %fusion.44 = f32[128,1792]{1,0:T(8,128)} fusion(bf16[128,4096]{1,0:T(8,128)(2,1)S(1)} %reshape.94, bf16[4096,1792]{1,0:T(8,128)(2,1)} %param.28), kind=kOutput, calls=%fused_computation.71 | convolution fusion | flops 1879048192 | bytes 16646144 | tf_op jit(solution)/shard_map/dot_general | solution.py:125
  274.2 8.2 %fusion.43 = f32[128,1792]{1,0:T(8,128)} fusion(bf16[128,4096]{1,0:T(8,128)(2,1)S(1)} %reshape.94, bf16[4096,1792]{1,0:T(8,128)(2,1)} %param.27), kind=kOutput, calls=%fused_computation.70 | convolution fusion | flops 1879048192 | bytes 16646144 | tf_op jit(solution)/shard_map/dot_general | solution.py:124
  282.5 19.7 %all-reduce.6.cloned.1.call-done = (f32[128,1792]{1,0:T(8,128)}, f32[128,1792]{1,0:T(8,128)}) async-done(((f32[128,1792]{1,0:T(8,128)}, f32[128,1792]{1,0:T(8,128)}), (f32[128,1792]{1,0:T(8,128)}, f32[128,1792]{1,0:T(8,128)})) %all-reduce.6.cloned.1.call-update) | async-done | bytes 1835024 | tf_op jit(solution)/shard_map/psum | solution.py:126
  302.3 9.2 %fusion.23 = f32[128,4096]{1,0:T(8,128)} fusion(bf16[1792,4096]{1,0:T(8,128)(2,1)} %param.29, f32[128,1792]{1,0:T(8,128)} %get-tuple-element.165, f32[128,1792]{1,0:T(8,128)} %get-tuple-element.166), kind=kOutput, calls=%fused_computation.42 | convolution fusion | flops 1880424448 | bytes 18612224 | tf_op jit(solution)/shard_map/dot_general | solution.py:129
  311.5 69.6 %reduce-scatter.2.cloned.1.call-done = f32[16,4096]{1,0:T(8,128)} async-done(((f32[128,4096]{1,0:T(8,128)}), f32[16,4096]{1,0:T(8,128)}) %reduce-scatter.2.cloned.1.call-update) | async-done | bytes 262160 | tf_op jit(solution)/shard_map/reduce_scatter | solution.py:128
  381.2 1.1 reshape.95
  (82 shorter events, 11.5 us)
Async XLA Ops:
  6.5 47.8 %copy-start.4 = (s32[64]{0:T(128)S(1)}, s32[64]{0:T(128)}, u32[]{:S(2)}) copy-start(s32[64]{0:T(128)} %param.25) | copy-start | bytes 772
  6.5 45.9 %all-gather.5.cloned.1.call-start = ((), (), s32[]{:S(2)}) async-start(), calls=%async_computation.2 | async-start | bytes 1179648 | tf_op jit(solution)/shard_map/all_gather | solution.py:61
  7.3 212.5 %all-reduce.4.cloned.1.call-start = ((), (), s32[]{:S(2)}) async-start(), calls=%async_computation.3 | async-start | bytes 4194304 | tf_op jit(solution)/shard_map/psum | solution.py:93
  114.1 0.9 copy-start
  114.1 1.7 copy-start.2
  114.1 33.8 %copy-start.3 = (bf16[8,2,512]{2,1,0:T(2,128)(2,1)S(1)}, bf16[8,2,512]{2,1,0:T(2,128)(2,1)}, u32[]{:S(2)}) copy-start(bf16[8,2,512]{2,1,0:T(2,128)(2,1)} %param.18) | copy-start | bytes 49156
  114.1 143.2 %all-gather.3.cloned.1.call-start = ((), (), s32[]{:S(2)}) async-start(), calls=%async_computation.1 | async-start | bytes 1179648 | tf_op jit(solution)/shard_map/all_gather | solution.py:64
  115.8 186.5 %all-reduce.6.cloned.1.call-start = ((), (), s32[]{:S(2)}) async-start(), calls=%async_computation.5 | async-start | bytes 3670016 | tf_op jit(solution)/shard_map/psum | solution.py:126
  225.8 36.4 %copy-start.1 = (f32[4096]{0:T(1024)S(1)}, f32[4096]{0:T(1024)}, u32[]{:S(2)}) copy-start(f32[4096]{0:T(1024)} %param.26) | copy-start | bytes 49156
  282.5 98.7 %reduce-scatter.2.cloned.1.call-start = ((), (), s32[]{:S(2)}) async-start(), calls=%async_computation.4 | async-start | bytes 2359296 | tf_op jit(solution)/shard_map/reduce_scatter | solution.py:128
Sparse Core Ops, SparseCore 0:
  9.5 42.9 all-gather.4
  114.2 100.8 all-reduce.3
  217.3 40.0 all-gather.2
  282.6 19.6 all-reduce.5
  311.6 69.4 reduce-scatter.1
where the time goes:
time: 390 us
  waiting for transfers between devices  164 us (42%)
  blocking collectives  134 us (34%)
  matrix products  50.9 us (13%)
  local copies, waits for them, and re-layouts  14.4 us (4%)
  between operations  13.3 us (3%)
  other arithmetic  12.1 us (3%)
    reduce_scatter x1, waiting for transfers between devices, body(): lax.psum_scatter(jnp.dot(hidden, w_down, preferred_element_type=jnp.float...  69.6 us
    all_gather x1, waiting for transfers between devices, body(): lax.all_gather(queries, 'seq', axis=0, tiled=True)  42.6 us
    pmax x1, blocking collectives, body(): row_peak = lax.pmax(partial_value[0], 'seq')  34.9 us
    psum x1, blocking collectives, body(): lax.psum((partial_value[1] * factor, partial_value[2] * factor[..., None]...  34.1 us
    all_gather x1, blocking collectives, body(): lax.all_gather(fresh_keys, 'seq', axis=0, tiled=True)  32 us
    all_gather x1, waiting for transfers between devices, body(): lax.all_gather(residual_in, 'seq', axis=0, tiled=True)  31.5 us
    all_gather x1, blocking collectives, body(): lax.all_gather(fresh_values, 'seq', axis=0, tiled=True)  30.8 us
    psum x1, waiting for transfers between devices, body(): gate_sums, up_sums = lax.psum((gate_part, up_part), 'tensor')  19.7 us
  transfers between devices with their start and end apart: 5, of which 4 were waited for; matrix products, arithmetic and copies ran while one was open for 4% of the time, Pallas kernels for 0%

commit v1 on v0

--- a/solution.py
+++ b/solution.py
@@ -1,8 +1,11 @@
+import functools
 import math
 
 import jax
 import jax.numpy as jnp
 from jax import lax
+from jax.experimental import pallas as pl
+from jax.experimental.pallas import tpu as pltpu
 from jax.sharding import PartitionSpec as P
 
 D = 8192
@@ -30,7 +33,7 @@
     return (row_top, exp_terms)
 
 
-def body(
+def plain_body(
     queries,
     fresh_keys,
     fresh_values,
@@ -134,6 +137,561 @@
     return (own_state + down_sums.reshape(local_rows, step_count, half_width)).astype(jnp.bfloat16)
 
 
+MESH = pl.DeviceIdType.MESH
+FLOOR = -1e29
+CHUNKS = 4
+W_PIECES = 4
+TILE = 256
+
+
+def layer_kernel(
+    lines,
+    steps,
+    q_ref,
+    fk_ref,
+    fv_ref,
+    res_ref,
+    lens_ref,
+    ks_ref,
+    vs_ref,
+    pt_ref,
+    gain_ref,
+    ck_hbm,
+    cv_hbm,
+    wg_hbm,
+    wu_hbm,
+    wd_hbm,
+    out_ref,
+    kbuf,
+    vbuf,
+    wgu,
+    wd,
+    qbuf,
+    krow,
+    vrow,
+    prow,
+    fkp,
+    fvp,
+    facc,
+    fstat,
+    part,
+    stat,
+    ypart,
+    ystat,
+    spart,
+    sstat,
+    zpart,
+    zstat,
+    hs,
+    sq,
+    nbuf,
+    gsend,
+    grecv,
+    gown,
+    hbuf,
+    dacc,
+    dpart,
+    dy,
+    dsum,
+    dz,
+    local_sem,
+    w_sem,
+    qz_sem,
+    qy_sem,
+    py_sem,
+    pz_sem,
+    sq_sem,
+    nz_sem,
+    ny_sem,
+    g_sem,
+    h_sem,
+    dy_sem,
+    dz_sem,
+):
+    f32 = jnp.float32
+    bf16 = jnp.bfloat16
+    seq = lax.axis_index("seq")
+    core = lax.axis_index("tensor")
+    z, y = seq // 2, lax.rem(seq, 2)
+    groups, span, hd = kbuf.shape
+    rows, width = q_ref.shape
+    heads = width // hd
+    per = heads // groups
+    pages = pt_ref.shape[1]
+    page = span // pages
+    inv_root = LOG2E / math.sqrt(hd)
+
+    def line(d):
+        return lax.rem(z + d, lines)
+
+    def to_y():
+        return {"seq": z * 2 + 1 - y}
+
+    def to_z(zz):
+        return {"seq": zz * 2 + y}
+
+    def to_core():
+        return {"tensor": 1 - core}
+
+    def remote(src, dst, sems, send_at, recv_at, where):
+        return pltpu.make_async_remote_copy(
+            src_ref=src,
+            dst_ref=dst,
+            send_sem=sems.at[0, send_at],
+            recv_sem=sems.at[1, recv_at],
+            device_id=where,
+            device_id_type=MESH,
+        )
+
+    cache_copies = [
+        pltpu.make_async_copy(ck_hbm, kbuf, local_sem.at[0]),
+        pltpu.make_async_copy(cv_hbm, vbuf, local_sem.at[1]),
+    ]
+    half = hbuf.shape[2]
+    weight_copies = []
+    for i, src in enumerate((wg_hbm, wu_hbm)):
+        for h in range(2):
+            piece = src.shape[0] // W_PIECES
+            for k in range(W_PIECES):
+                at = pl.ds(k * piece, piece)
+                weight_copies.append(
+                    pltpu.make_async_copy(
+                        src.at[at, pl.ds(h * half, half)],
+                        wgu.at[h, at, pl.ds(i * half, half)],
+                        w_sem.at[2 * i + h, k],
+                    )
+                )
+    down_copies = []
+    for k in range(W_PIECES):
+        piece = wd_hbm.shape[0] // W_PIECES
+        at = pl.ds(k * piece, piece)
+        down_copies.append(pltpu.make_async_copy(wd_hbm.at[at], wd.at[at], w_sem.at[4, k]))
+    for copy in cache_copies:
+        copy.start()
+
+    qbuf[y, z] = q_ref[...]
+
+    barrier = pltpu.get_barrier_semaphore()
+    peers = [to_y(), to_core()] + [to_z(line(d)) for d in range(1, lines)]
+    for where in peers:
+        pl.semaphore_signal(barrier, inc=1, device_id=where, device_id_type=MESH)
+    pl.semaphore_wait(barrier, len(peers))
+
+    def gather_z(buf, sems, d):
+        return remote(buf.at[y, z], buf.at[y, z], sems, d, z, to_z(line(d)))
+
+    def gather_z_arrival(buf, sems, zz):
+        return remote(buf.at[y, zz], buf.at[y, zz], sems, 0, zz, to_z(zz))
+
+    def gather_y(buf, sems, zz):
+        return remote(buf.at[y, zz], buf.at[y, zz], sems, zz, zz, to_y())
+
+    def gather_y_arrival(buf, sems, zz):
+        return remote(buf.at[1 - y, zz], buf.at[1 - y, zz], sems, zz, zz, to_y())
+
+    gather_y(qbuf, qy_sem, z).start()
+    for d in range(1, lines):
+        gather_z(qbuf, qz_sem, d).start()
+    for copy in weight_copies + down_copies:
+        copy.start()
+
+    owner = lax.broadcasted_iota(jnp.int32, (1, span), 1) // page
+    within = lax.rem(lax.broadcasted_iota(jnp.int32, (1, span), 1), page)
+    place = jnp.zeros((1, span), jnp.int32)
+    for j in range(pages):
+        place = jnp.where(owner == j, pt_ref[:, j : j + 1], place)
+    prow[...] = (seq * pages + place) * page + within
+    for g in range(groups):
+        k_line = jnp.zeros((1, span), f32)
+        v_line = jnp.zeros((1, span), f32)
+        for j in range(pages):
+            k_line = jnp.where(owner == j, ks_ref[g : g + 1, j : j + 1], k_line)
+            v_line = jnp.where(owner == j, vs_ref[g : g + 1, j : j + 1], v_line)
+        krow[g] = k_line * inv_root
+        vrow[g] = v_line
+
+    lane = lax.broadcasted_iota(jnp.int32, (rows, 128), 1)
+
+    def stacked(block, g):
+        return jnp.concatenate(
+            [block[:, (g * per + j) * hd : (g * per + j + 1) * hd] for j in range(per)], axis=0
+        )
+
+    def softmax_terms(scores):
+        top = jnp.maximum(jnp.ceil(jnp.max(scores, axis=-1, keepdims=True)), FLOOR)
+        terms = jnp.exp2(scores - top)
+        return top, terms, jnp.sum(terms, axis=-1, keepdims=True)
+
+    def spread(tops, totals, g, top, total):
+        for j in range(per):
+            at = slice(j * rows, (j + 1) * rows)
+            tops = jnp.where(lane == g * per + j, top[at], tops)
+            totals = jnp.where(lane == g * per + j, total[at], totals)
+        return tops, totals
+
+    fkp[...] = jnp.zeros_like(fkp)
+    fvp[...] = jnp.zeros_like(fvp)
+    fkp[0:rows] = fk_ref[...]
+    fvp[0:rows] = fv_ref[...]
+    slots = fkp.shape[0]
+    token = lax.rem(lax.broadcasted_iota(jnp.int32, (per * rows, slots), 0), rows)
+    key_token = lax.broadcasted_iota(jnp.int32, (per * rows, slots), 1)
+    allowed = (token // steps == key_token // steps) & (key_token <= token)
+    tops, totals = jnp.zeros((rows, 128), f32), jnp.ones((rows, 128), f32)
+    for g in range(groups):
+        scores = lax.dot_general(
+            stacked(q_ref, g),
+            fkp[:, g * hd : (g + 1) * hd],
+            (((1,), (1,)), ((), ())),
+            preferred_element_type=f32,
+        )
+        top, terms, total = softmax_terms(jnp.where(allowed, scores * inv_root, NEG_FILL))
+        acc = jnp.dot(
+            terms.astype(bf16), fvp[:, g * hd : (g + 1) * hd], preferred_element_type=f32
+        )
+        for j in range(per):
+            facc[:, (g * per + j) * hd : (g * per + j + 1) * hd] = acc[j * rows : (j + 1) * rows]
+        tops, totals = spread(tops, totals, g, top, total)
+    fstat[0] = tops
+    fstat[1] = totals
+
+    for copy in cache_copies:
+        copy.wait()
+
+    def attend(yy, zz):
+        lens = jnp.concatenate([lens_ref[yy, zz]] * per, axis=0)
+        block = qbuf.at[yy, zz]
+        out = part.at[yy, zz]
+        tops, totals = jnp.zeros((rows, 128), f32), jnp.ones((rows, 128), f32)
+        for g in range(groups):
+            scores = lax.dot_general(
+                stacked(block, g), kbuf[g], (((1,), (1,)), ((), ())), preferred_element_type=f32
+            )
+            scores = jnp.where(prow[...] < lens, scores * krow[g], NEG_FILL)
+            top, terms, total = softmax_terms(scores)
+            acc = jnp.dot(
+                (terms * vrow[g]).astype(bf16), vbuf[g], preferred_element_type=f32
+            ).astype(bf16)
+            for j in range(per):
+                out[:, (g * per + j) * hd : (g * per + j + 1) * hd] = acc[j * rows : (j + 1) * rows]
+            tops, totals = spread(tops, totals, g, top, total)
+        stat[yy, zz, 0] = tops
+        stat[yy, zz, 1] = totals
+
+    def part_y(zz):
+        src = (part.at[1 - y, zz], stat.at[1 - y, zz])
+        dst = (ypart.at[zz], ystat.at[zz])
+        return [remote(src[i], dst[i], py_sem, i * lines + zz, i * lines + zz, to_y()) for i in range(2)]
+
+    def part_z(zz, at):
+        src, dst = (spart.at[zz], sstat.at[zz]), (zpart.at[at], zstat.at[at])
+        return [
+            remote(src[i], dst[i], pz_sem, i * lines + zz, i * lines + at, to_z(zz)) for i in range(2)
+        ]
+
+    def join(zz):
+        for copy in part_y(zz):
+            copy.wait_recv()
+        first, second = stat[y, zz, 0], ystat[zz, 0]
+        top = jnp.maximum(first, second)
+        a, b = jnp.exp2(first - top), jnp.exp2(second - top)
+        sstat[zz, 0] = top
+        sstat[zz, 1] = stat[y, zz, 1] * a + ystat[zz, 1] * b
+        for h in range(heads):
+            at = slice(h * hd, (h + 1) * hd)
+            spart[zz, :, at] = (
+                part[y, zz, :, at].astype(f32) * a[:, h : h + 1]
+                + ypart[zz, :, at].astype(f32) * b[:, h : h + 1]
+            ).astype(bf16)
+        for copy in part_z(zz, z):
+            copy.start()
+
+    @pl.loop(0, 2 * lines)
+    def _(k):
+        d, other = k // 2, lax.rem(k, 2)
+        zz = line(d)
+
+        @pl.when((other == 0) & (d > 0))
+        def _():
+            gather_z_arrival(qbuf, qz_sem, zz).wait_recv()
+            gather_y(qbuf, qy_sem, zz).start()
+
+        @pl.when(other == 1)
+        def _():
+            gather_y_arrival(qbuf, qy_sem, zz).wait_recv()
+
+        attend(lax.rem(y + other, 2), zz)
+
+        @pl.when(other == 1)
+        def _():
+            for copy in part_y(zz):
+                copy.start()
+
+        @pl.when((other == 1) & (d > 1))
+        def _():
+            join(line(d - 1))
+
+    join(line(lines - 1))
+    for copy in part_y(z):
+        copy.wait_recv()
+
+    for d in range(1, lines):
+        for copy in part_z(line(d), line(d)):
+            copy.wait_recv()
+    stats = [fstat, stat.at[y, z], ystat.at[z]] + [zstat.at[line(d)] for d in range(1, lines)]
+    parts = [facc, part.at[y, z], ypart.at[z]] + [zpart.at[line(d)] for d in range(1, lines)]
+    top = functools.reduce(jnp.maximum, [s[0] for s in stats])
+    factors = [jnp.exp2(s[0] - top) for s in stats]
+    total = sum(s[1] * f for s, f in zip(stats, factors))
+    factors = [f / total for f in factors]
+    square = jnp.zeros((rows, hd), f32)
+    for h in range(heads):
+        at = slice(h * hd, (h + 1) * hd)
+        state = res_ref[:, at].astype(f32) + sum(
+            p[:, at].astype(f32) * f[:, h : h + 1] for p, f in zip(parts, factors)
+        )
+        hs[:, at] = state
+        square += state * state
+    sq[0] = jnp.broadcast_to(jnp.sum(square, axis=-1, keepdims=True), (rows, 128))
+    square_copy = remote(sq.at[0], sq.at[1], sq_sem, 0, 0, to_core())
+    square_copy.start()
+    square_copy.wait_recv()
+    inverse = lax.rsqrt((sq[0] + sq[1])[:, 0:1] / (2 * width) + EPSILON)
+    nbuf[y, z] = (hs[...] * inverse * gain_ref[...]).astype(bf16)
+
+    gather_y(nbuf, ny_sem, z).start()
+    for d in range(1, lines):
+        gather_z(nbuf, nz_sem, d).start()
+    for d in range(1, lines):
+        gather_z_arrival(nbuf, nz_sem, line(d)).wait_recv()
+        gather_y(nbuf, ny_sem, line(d)).start()
+    for copy in weight_copies:
+        copy.wait()
+    for d in range(lines):
+        gather_y_arrival(nbuf, ny_sem, line(d)).wait_recv()
+
+    all_rows = 2 * lines * rows
+
+    def gate_up(at, out):
+        @pl.loop(0, 2 * half // TILE)
+        def _(t):
+            columns = pl.ds(pl.multiple_of(t * TILE, TILE), TILE)
+            out[:, columns] = jnp.dot(
+                nbuf[...].reshape(all_rows, width),
+                wgu[at, :, columns],
+                preferred_element_type=f32,
+            ).astype(out.dtype)
+
+    exchange = remote(gsend, grecv, g_sem, 0, 0, to_core())
+    gate_up(1 - core, gsend)
+    exchange.start()
+    gate_up(core, gown)
+    exchange.wait_recv()
+    gate = gown[:, :half] + grecv[:, :half].astype(f32)
+    up = gown[:, half:] + grecv[:, half:].astype(f32)
+    hbuf[core] = (gate / (1.0 + jnp.exp(-gate)) * up).astype(bf16)
+    hidden_copy = remote(hbuf.at[core], hbuf.at[core], h_sem, 0, 0, to_core())
+    hidden_copy.start()
+
+    chunk = width // CHUNKS
+    for copy in down_copies:
+        copy.wait()
+
+    def down(at, c, add):
+        @pl.loop(0, chunk // TILE)
+        def _(t):
+            columns = pl.ds(pl.multiple_of(t * TILE, TILE), TILE)
+            value = jnp.dot(
+                hbuf[at],
+                wd[
+                    pl.ds(pl.multiple_of(at * half, 128), half),
+                    pl.ds(pl.multiple_of(c * chunk + t * TILE, TILE), TILE),
+                ],
+                preferred_element_type=f32,
+            ).reshape(2, lines, rows, TILE)
+            if add:
+                value += dacc[c, :, :, :, columns]
+            dacc[c, :, :, :, columns] = value
+
+    for c in range(CHUNKS):
+        down(core, c, False)
+    remote(hbuf.at[1 - core], hbuf.at[1 - core], h_sem, 0, 0, to_core()).wait_recv()
+
+    def down_y(c):
+        return remote(dpart.at[c], dy.at[c], dy_sem, c, c, to_y())
+
+    def down_z(c, zz, at):
+        return remote(
+            dsum.at[c, zz], dz.at[c, at], dz_sem, c * lines + zz, c * lines + at, to_z(zz)
+        )
+
+    def relay(c):
+        down_y(c).wait_recv()
+        for d in range(1, lines):
+            zz = line(d)
+            dsum[c, zz] = (dacc[c, y, zz] + dy[c, zz].astype(f32)).astype(bf16)
+            down_z(c, zz, z).start()
+
+    for c in range(CHUNKS):
+        down(1 - core, c, True)
+        dpart[c] = dacc[c, 1 - y].astype(bf16)
+        down_y(c).start()
+        if c > 0:
+            relay(c - 1)
+    relay(CHUNKS - 1)
+    for c in range(CHUNKS):
+        at = slice(c * chunk, (c + 1) * chunk)
+        value = hs[:, at] + dacc[c, y, z] + dy[c, z].astype(f32)
+        for d in range(1, lines):
+            down_z(c, line(d), line(d)).wait_recv()
+            value += dz[c, line(d)].astype(f32)
+        out_ref[:, at] = value.astype(out_ref.dtype)
+
+    for d in range(1, lines):
+        gather_z(qbuf, qz_sem, d).wait_send()
+        gather_z(nbuf, nz_sem, d).wait_send()
+        for copy in part_z(line(d), z):
+            copy.wait_send()
+        for c in range(CHUNKS):
+            down_z(c, line(d), z).wait_send()
+    for d in range(lines):
+        gather_y(qbuf, qy_sem, line(d)).wait_send()
+        gather_y(nbuf, ny_sem, line(d)).wait_send()
+        for copy in part_y(line(d)):
+            copy.wait_send()
+    for c in range(CHUNKS):
+        down_y(c).wait_send()
+    square_copy.wait_send()
+    hidden_copy.wait_send()
+    exchange.wait_send()
+
+
+def kernel_body(
+    lines,
+    queries,
+    fresh_keys,
+    fresh_values,
+    residual_in,
+    cache_keys,
+    cache_values,
+    key_scales,
+    value_scales,
+    page_table,
+    row_lengths,
+    norm_gain,
+    w_gate,
+    w_up,
+    w_down,
+):
+    local_rows, steps, width = queries.shape
+    groups, span, hd = cache_keys.shape
+    rows = local_rows * steps
+    fresh_width = fresh_keys.shape[2]
+    half = w_gate.shape[1] // 2
+    chunk = width // CHUNKS
+    all_rows = 2 * lines * rows
+    lens = row_lengths.reshape(lines, 2, local_rows, 1).transpose(1, 0, 2, 3)
+    lens = jnp.broadcast_to(lens, (2, lines, local_rows, steps)).reshape(2, lines, rows, 1)
+    bf16, f32 = jnp.bfloat16, jnp.float32
+    vmem = pl.BlockSpec(memory_space=pltpu.VMEM)
+    anywhere = pl.BlockSpec(memory_space=pl.ANY)
+    dma = pltpu.SemaphoreType.DMA
+    out = pl.pallas_call(
+        functools.partial(layer_kernel, lines, steps),
+        out_shape=jax.ShapeDtypeStruct((rows, width), bf16),
+        in_specs=[vmem] * 9 + [anywhere] * 5,
+        out_specs=vmem,
+        scratch_shapes=[
+            pltpu.VMEM((groups, span, hd), bf16),
+            pltpu.VMEM((groups, span, hd), bf16),
+            pltpu.VMEM((2, width, 2 * half), bf16),
+            pltpu.VMEM(w_down.shape, bf16),
+            pltpu.VMEM((2, lines, rows, width), bf16),
+            pltpu.VMEM((groups, 1, span), f32),
+            pltpu.VMEM((groups, 1, span), f32),
+            pltpu.VMEM((1, span), jnp.int32),
+            pltpu.VMEM((128, fresh_width), bf16),
+            pltpu.VMEM((128, fresh_width), bf16),
+            pltpu.VMEM((rows, width), f32),
+            pltpu.VMEM((2, rows, 128), f32),
+            pltpu.VMEM((2, lines, rows, width), bf16),
+            pltpu.VMEM((2, lines, 2, rows, 128), f32),
+            pltpu.VMEM((lines, rows, width), bf16),
+            pltpu.VMEM((lines, 2, rows, 128), f32),
+            pltpu.VMEM((lines, rows, width), bf16),
+            pltpu.VMEM((lines, 2, rows, 128), f32),
+            pltpu.VMEM((lines, rows, width), bf16),
+            pltpu.VMEM((lines, 2, rows, 128), f32),
+            pltpu.VMEM((rows, width), f32),
+            pltpu.VMEM((2, rows, 128), f32),
+            pltpu.VMEM((2, lines, rows, width), bf16),
+            pltpu.VMEM((all_rows, 2 * half), bf16),
+            pltpu.VMEM((all_rows, 2 * half), bf16),
+            pltpu.VMEM((all_rows, 2 * half), f32),
+            pltpu.VMEM((2, all_rows, half), bf16),
+            pltpu.VMEM((CHUNKS, 2, lines, rows, chunk), f32),
+            pltpu.VMEM((CHUNKS, lines, rows, chunk), bf16),
+            pltpu.VMEM((CHUNKS, lines, rows, chunk), bf16),
+            pltpu.VMEM((CHUNKS, lines, rows, chunk), bf16),
+            pltpu.VMEM((CHUNKS, lines, rows, chunk), bf16),
+            dma((2,)),
+            dma((5, W_PIECES)),
+            dma((2, lines)),
+            dma((2, lines)),
+            dma((2, 2 * lines)),
+            dma((2, 2 * lines)),
+            dma((2, 1)),
+            dma((2, lines)),
+            dma((2, lines)),
+            dma((2, 1)),
+            dma((2, 1)),
+            dma((2, CHUNKS)),
+            dma((2, CHUNKS * lines)),
+        ],
+        compiler_params=pltpu.CompilerParams(
+            collective_id=0, has_side_effects=True, vmem_limit_bytes=60 * 1024 * 1024
+        ),
+    )(
+        queries.reshape(rows, width),
+        fresh_keys.reshape(rows, fresh_width),
+        fresh_values.reshape(rows, fresh_width),
+        residual_in.reshape(rows, width),
+        lens,
+        key_scales,
+        value_scales,
+        page_table,
+        norm_gain.reshape(1, width),
+        cache_keys,
+        cache_values,
+        w_gate,
+        w_up,
+        w_down,
+    )
+    return out.reshape(local_rows, steps, width)
+
+
+def choose_body(seq_size, cores, *args):
+    local_rows, steps, width = args[0].shape
+    head_dim = args[4].shape[2]
+    rows, hidden = local_rows * steps, args[11].shape[1]
+    heads = width // head_dim
+    weights = 2 * 3 * width * hidden
+    fits = (
+        cores == 2
+        and seq_size % 2 == 0
+        and rows % 16 == 0
+        and rows <= 128
+        and hidden % 256 == 0
+        and width % (CHUNKS * TILE) == 0
+        and head_dim == 128
+        and heads <= 128
+        and weights <= 44 * 1024 * 1024
+    )
+    if fits:
+        return kernel_body(seq_size // 2, *args)
+    return plain_body(*args)
+
+
 def solution(mesh):
     in_specs = (
         P(("groups", "seq"), None, "tensor"),
@@ -152,4 +710,5 @@
         P("seq", "tensor"),
     )
     out_specs = P(("groups", "seq"), None, "tensor")
+    body = functools.partial(choose_body, mesh.shape["seq"], mesh.shape["tensor"])
     return jax.shard_map(body, mesh=mesh, in_specs=in_specs, out_specs=out_specs, check_vma=False)

time: 390 us -> 115 us (0.29)
  waiting for transfers between devices: 164 us -> 0 us
  blocking collectives: 134 us -> 0 us
  Pallas kernels: 0 us -> 105 us
  matrix products: 50.9 us -> 0 us
  between operations: 13.3 us -> 0.01 us
  other arithmetic: 12.1 us -> 0 us
  local copies, waits for them, and re-layouts: 14.4 us -> 9.29 us
    pallas_call x0 -> x1, Pallas kernels: none -> 105 us  [kernel_body(): pl.pallas_call(functools.partial(layer_kernel, lines, steps), out_shape=j...]
    all_gather x2 -> x0, waiting for transfers between devices: 74.2 us -> none  [the longest x1 42.6 us: body(): lax.all_gather(queries, 'seq', axis=0, tiled=True)]
    reduce_scatter x1 -> x0, waiting for transfers between devices: 69.6 us -> none  [body(): lax.psum_scatter(jnp.dot(hidden, w_down, preferred_element_type=jnp.float...]
    all_gather x2 -> x0, blocking collectives: 62.8 us -> none  [the longest x1 32 us: body(): lax.all_gather(fresh_keys, 'seq', axis=0, tiled=True)]
    dot_general x13 -> x0, matrix products: 50.9 us -> none  [the longest x4 10.1 us: per_group(): jnp.einsum('nsqc,cd->nsqd', weights, value_block, preferred_element_type=...]
    psum x2 -> x0, blocking collectives: 36.7 us -> none  [the longest x1 34.1 us: body(): lax.psum((partial_value[1] * factor, partial_value[2] * factor[..., None]...]
    pmax x1 -> x0, blocking collectives: 34.9 us -> none  [body(): row_peak = lax.pmax(partial_value[0], 'seq')]
    psum x2 -> x0, waiting for transfers between devices: 19.8 us -> none  [the longest x1 19.7 us: body(): gate_sums, up_sums = lax.psum((gate_part, up_part), 'tensor')]
  transfers between devices with their start and end apart: 5 -> 0, of which waited for: 4 -> 0; matrix products, arithmetic and copies ran while one was open for 4% -> 0% of each run, Pallas kernels for 0% -> 0%
where the time goes in v1:
time: 115 us; the launch traced here: 114 us
  Pallas kernels  105 us (91%)
  local copies, waits for them, and re-layouts  9.29 us (8%)
    pallas_call x1, Pallas kernels, kernel_body(): pl.pallas_call(functools.partial(layer_kernel, lines, steps), out_shape=j...  105 us

profile of v1, /device:TPU:0, one launch (start us, length us, event | category | flops | bytes accessed | tf_op | source)
XLA Modules:
  0.0 114.4 jit_solution(4989319551971735854)
XLA Ops:
  0.0 0.7 reshape.28
  0.7 0.1 copy.16
  0.8 1.3 %reshape.25.fk_ref = bf16[16,512]{1,0:T(8,128)(2,1)} reshape(bf16[8,2,512]{2,1,0:T(2,128)(2,1)} %param.15) | data formatting | bytes 32768 | tf_op jit(solution)/shard_map/reshape | solution.py:656
  2.2 1.3 %reshape.26.fv_ref = bf16[16,512]{1,0:T(8,128)(2,1)} reshape(bf16[8,2,512]{2,1,0:T(2,128)(2,1)} %param.16) | data formatting | bytes 32768 | tf_op jit(solution)/shard_map/reshape | solution.py:657
  3.5 0.9 copy.17.lens_ref
  4.4 1.6 %reshape.24.q_ref = bf16[16,4096]{1,0:T(8,128)(2,1)} reshape(bf16[8,2,4096]{2,1,0:T(2,128)(2,1)} %param.14) | data formatting | bytes 262144 | tf_op jit(solution)/shard_map/reshape | solution.py:655
  6.0 1.6 %reshape.27.res_ref = bf16[16,4096]{1,0:T(8,128)(2,1)} reshape(bf16[8,2,4096]{2,1,0:T(2,128)(2,1)} %param.17) | data formatting | bytes 262144 | tf_op jit(solution)/shard_map/reshape | solution.py:658
  7.6 105.1 %shard_map.136 = bf16[16,4096]{1,0:T(8,128)(2,1)} custom-call(bf16[16,4096]{1,0:T(8,128)(2,1)} %reshape.24.q_ref, bf16[16,512]{1,0:T(8,128)(2,1)} %reshape.25.fk_ref, bf16[16,512]{1,0:T(8,128)(2,1)} %reshape.26.fv_ref, bf16[16,4096]{1,0:T(8,128)(2,1)} %reshape.27.res_ref, s32[2,4,16,1]{3,2,1,0:T(8,128)} %copy.17.lens_ref, f32[4,8]{1,0:T(4,128)} %ks_ref.1, ...), custom_call_target="tpu_custom_call" | custom-call | tf_op jit(solution)/shard_map/pallas_call | solution.py:599
  112.7 1.7 %reshape.31 = bf16[8,2,4096]{2,1,0:T(2,128)(2,1)} reshape(bf16[16,4096]{1,0:T(8,128)(2,1)} %shard_map.136) | data formatting | bytes 262144 | tf_op jit(solution)/shard_map/reshape | solution.py:670
  (1 shorter events, 0.0 us)

commit v2 on v0

--- a/solution.py
+++ b/solution.py
@@ -1,8 +1,11 @@
+import functools
 import math
 
 import jax
 import jax.numpy as jnp
 from jax import lax
+from jax.experimental import pallas as pl
+from jax.experimental.pallas import tpu as pltpu
 from jax.sharding import PartitionSpec as P
 
 D = 8192
@@ -30,7 +33,7 @@
     return (row_top, exp_terms)
 
 
-def body(
+def plain_body(
     queries,
     fresh_keys,
     fresh_values,
@@ -134,6 +137,618 @@
     return (own_state + down_sums.reshape(local_rows, step_count, half_width)).astype(jnp.bfloat16)
 
 
+MESH = pl.DeviceIdType.MESH
+FLOOR = -1e29
+CHUNKS = 8
+TILE = 256
+LAG = 3
+
+
+def layer_kernel(
+    lines,
+    q_ref,
+    fk_ref,
+    fv_ref,
+    res_ref,
+    lens_ref,
+    ks_ref,
+    vs_ref,
+    pt_ref,
+    gain_ref,
+    ck_hbm,
+    cv_hbm,
+    wg_hbm,
+    wu_hbm,
+    wd_hbm,
+    out_ref,
+    kbuf,
+    vbuf,
+    wgu,
+    wd,
+    qbuf,
+    lens,
+    krow,
+    vrow,
+    prow,
+    fkp,
+    fvp,
+    facc,
+    fstat,
+    part,
+    stat,
+    ypart,
+    ystat,
+    spart,
+    sstat,
+    zpart,
+    zstat,
+    hs,
+    sq,
+    nbuf,
+    gacc,
+    grecv,
+    hbuf,
+    dacc,
+    dpart,
+    dy,
+    dsum,
+    dz,
+    local_sem,
+    w_sem,
+    qz_sem,
+    qy_sem,
+    py_sem,
+    pz_sem,
+    sq_sem,
+    nz_sem,
+    ny_sem,
+    g_sem,
+    h_sem,
+    dy_sem,
+    dz_sem,
+):
+    f32 = jnp.float32
+    bf16 = jnp.bfloat16
+    seq = lax.axis_index("seq")
+    core = lax.axis_index("tensor")
+    z, y = seq // 2, lax.rem(seq, 2)
+    groups, span, hd = kbuf.shape
+    local_rows, steps, width = q_ref.shape
+    rows = local_rows * steps
+    group_width = width // groups
+    per = group_width // hd
+    stack = per * rows
+    pages = pt_ref.shape[1]
+    page = span // pages
+    inv_root = LOG2E / math.sqrt(hd)
+    half = hbuf.shape[1] // 2
+    pairs = groups * lines
+
+    def line(d):
+        return lax.rem(z + d, lines)
+
+    def to_y():
+        return {"seq": z * 2 + 1 - y}
+
+    def to_z(zz):
+        return {"seq": zz * 2 + y}
+
+    def to_core():
+        return {"tensor": 1 - core}
+
+    def remote(src, dst, sems, send_at, recv_at, where):
+        return pltpu.make_async_remote_copy(
+            src_ref=src,
+            dst_ref=dst,
+            send_sem=sems.at[(0,) + send_at],
+            recv_sem=sems.at[(1,) + recv_at],
+            device_id=where,
+            device_id_type=MESH,
+        )
+
+    cache_copies = [
+        pltpu.make_async_copy(ck_hbm, kbuf, local_sem.at[0]),
+        pltpu.make_async_copy(cv_hbm, vbuf, local_sem.at[1]),
+    ]
+
+    def gate_up_copies(p):
+        piece = width // pairs
+        at = pl.ds(pl.multiple_of(p * piece, 16), piece)
+        return [
+            pltpu.make_async_copy(
+                src.at[at, pl.ds(h * half, half)],
+                wgu.at[h, at, pl.ds(i * half, half)],
+                w_sem.at[2 * i + h, p],
+            )
+            for i, src in enumerate((wg_hbm, wu_hbm))
+            for h in range(2)
+        ]
+
+    def down_copy(p):
+        piece = wd_hbm.shape[0] // pairs
+        at = pl.ds(pl.multiple_of(p * piece, 16), piece)
+        return pltpu.make_async_copy(wd_hbm.at[at], wd.at[at], w_sem.at[4, p])
+
+    for copy in cache_copies:
+        copy.start()
+
+    barrier = pltpu.get_barrier_semaphore()
+    peers = [to_y(), to_core()] + [to_z(line(d)) for d in range(1, lines)]
+    for where in peers:
+        pl.semaphore_signal(barrier, inc=1, device_id=where, device_id_type=MESH)
+
+    flat_q = q_ref[...].reshape(rows, width)
+    for g in range(groups):
+        qbuf[g, y, z] = flat_q[:, g * group_width : (g + 1) * group_width]
+    pl.semaphore_wait(barrier, len(peers))
+
+    def gather_z(buf, sems, g, d):
+        return remote(buf.at[g, y, z], buf.at[g, y, z], sems, (g, d), (g, z), to_z(line(d)))
+
+    def gather_z_arrival(buf, sems, g, zz):
+        return remote(buf.at[g, y, zz], buf.at[g, y, zz], sems, (g, 0), (g, zz), to_z(zz))
+
+    def gather_y(buf, sems, g, zz):
+        return remote(buf.at[g, y, zz], buf.at[g, y, zz], sems, (g, zz), (g, zz), to_y())
+
+    def gather_y_arrival(buf, sems, g, zz):
+        return remote(buf.at[g, 1 - y, zz], buf.at[g, 1 - y, zz], sems, (g, zz), (g, zz), to_y())
+
+    for g in range(groups):
+        gather_y(qbuf, qy_sem, g, z).start()
+        for d in range(1, lines):
+            gather_z(qbuf, qz_sem, g, d).start()
+
+    row_of = lax.rem(lax.broadcasted_iota(jnp.int32, (stack, 1), 0), rows) // steps
+
+    @pl.loop(0, 2 * lines)
+    def _(k):
+        yy, zz = lax.rem(k, 2), k // 2
+        value = jnp.zeros((stack, 1), jnp.int32)
+        for r in range(local_rows):
+            value = jnp.where(row_of == r, lens_ref[k * local_rows + r], value)
+        lens[yy, zz] = value
+
+    owner = lax.broadcasted_iota(jnp.int32, (1, span), 1) // page
+    within = lax.rem(lax.broadcasted_iota(jnp.int32, (1, span), 1), page)
+    place = jnp.zeros((1, span), jnp.int32)
+    for j in range(pages):
+        place = jnp.where(owner == j, pt_ref[:, j : j + 1], place)
+    prow[...] = (seq * pages + place) * page + within
+    for g in range(groups):
+        k_line = jnp.zeros((1, span), f32)
+        v_line = jnp.zeros((1, span), f32)
+        for j in range(pages):
+            k_line = jnp.where(owner == j, ks_ref[g : g + 1, j : j + 1], k_line)
+            v_line = jnp.where(owner == j, vs_ref[g : g + 1, j : j + 1], v_line)
+        krow[g] = k_line * inv_root
+        vrow[g] = v_line
+
+    lane = lax.broadcasted_iota(jnp.int32, (stack, 128), 1)
+    sublane = lax.broadcasted_iota(jnp.int32, (128, stack), 0)
+
+    def stacked(block):
+        return jnp.concatenate([block[:, j * hd : (j + 1) * hd] for j in range(per)], axis=0)
+
+    def softmax_terms(scores):
+        top = jnp.maximum(jnp.ceil(jnp.max(scores, axis=-1, keepdims=True)), FLOOR)
+        terms = jnp.exp2(scores - top)
+        total = jnp.sum(terms, axis=-1, keepdims=True)
+        return terms, jnp.where(lane == 0, top, total).T[0:2]
+
+    def columns_of(lines_in):
+        table = jnp.zeros((128, stack), f32)
+        for i, value in enumerate(lines_in):
+            table = jnp.where(sublane == i, value, table)
+        table = table.T
+        return [table[:, i : i + 1] for i in range(len(lines_in))]
+
+    fkp[...] = jnp.zeros_like(fkp)
+    fvp[...] = jnp.zeros_like(fvp)
+    fkp[0:rows] = fk_ref[...].reshape(rows, groups * hd)
+    fvp[0:rows] = fv_ref[...].reshape(rows, groups * hd)
+    slots = fkp.shape[0]
+    token = lax.rem(lax.broadcasted_iota(jnp.int32, (stack, slots), 0), rows)
+    key_token = lax.broadcasted_iota(jnp.int32, (stack, slots), 1)
+    allowed = (token // steps == key_token // steps) & (key_token <= token)
+    for g in range(groups):
+        at = slice(g * hd, (g + 1) * hd)
+        scores = lax.dot_general(
+            stacked(qbuf.at[g, y, z]),
+            fkp[:, at],
+            (((1,), (1,)), ((), ())),
+            preferred_element_type=f32,
+        )
+        terms, fstat[g] = softmax_terms(jnp.where(allowed, scores * inv_root, NEG_FILL))
+        facc[g] = jnp.dot(terms.astype(bf16), fvp[:, at], preferred_element_type=f32)
+    flat_res = res_ref[...].reshape(rows, width)
+    for g in range(groups):
+        hs[g] = flat_res[:, g * group_width : (g + 1) * group_width].astype(f32)
+    gacc[...] = jnp.zeros_like(gacc)
+
+    for copy in cache_copies:
+        copy.wait()
+
+    def attend(g, yy, zz):
+        scores = lax.dot_general(
+            stacked(qbuf.at[g, yy, zz]),
+            kbuf[g],
+            (((1,), (1,)), ((), ())),
+            preferred_element_type=f32,
+        )
+        scores = jnp.where(prow[...] < lens[yy, zz], scores * krow[g], NEG_FILL)
+        terms, stat[g, yy, zz] = softmax_terms(scores)
+        part[g, yy, zz] = jnp.dot(
+            (terms * vrow[g]).astype(bf16), vbuf[g], preferred_element_type=f32
+        ).astype(bf16)
+
+    def part_y(g, zz):
+        src = (part.at[g, 1 - y, zz], stat.at[g, 1 - y, zz])
+        dst = (ypart.at[g, zz], ystat.at[g, zz])
+        return [remote(src[i], dst[i], py_sem, (i, g, zz), (i, g, zz), to_y()) for i in range(2)]
+
+    def part_z(g, zz, at):
+        src, dst = (spart.at[g, zz], sstat.at[g, zz]), (zpart.at[g, at], zstat.at[g, at])
+        return [remote(src[i], dst[i], pz_sem, (i, g, zz), (i, g, at), to_z(zz)) for i in range(2)]
+
+    def join(g, zz):
+        for copy in part_y(g, zz):
+            copy.wait_recv()
+        first, second = stat[g, y, zz], ystat[g, zz]
+        top = jnp.maximum(first[0:1], second[0:1])
+        a, b = jnp.exp2(first[0:1] - top), jnp.exp2(second[0:1] - top)
+        sstat[g, zz, 0:1] = top
+        sstat[g, zz, 1:2] = first[1:2] * a + second[1:2] * b
+        a, b = columns_of([a, b])
+        spart[g, zz] = (part[g, y, zz].astype(f32) * a + ypart[g, zz].astype(f32) * b).astype(bf16)
+        for copy in part_z(g, zz, z):
+            copy.start()
+
+    @pl.loop(0, 2 * pairs)
+    def _(k):
+        pair, other = k // 2, lax.rem(k, 2)
+        g, d = pair // lines, lax.rem(pair, lines)
+        zz = line(d)
+
+        @pl.when(other == 0)
+        def _():
+            for copy in gate_up_copies(pair) + [down_copy(pair)]:
+                copy.start()
+
+        @pl.when((other == 0) & (d > 0))
+        def _():
+            gather_z_arrival(qbuf, qz_sem, g, zz).wait_recv()
+            gather_y(qbuf, qy_sem, g, zz).start()
+
+        @pl.when(other == 1)
+        def _():
+            gather_y_arrival(qbuf, qy_sem, g, zz).wait_recv()
+
+        attend(g, lax.rem(y + other, 2), zz)
+
+        @pl.when(other == 1)
+        def _():
+            for copy in part_y(g, zz):
+                copy.start()
+
+        late = pair + lines - LAG
+
+        @pl.when((other == 1) & (late >= lines) & (lax.rem(late, lines) > 0))
+        def _():
+            join(late // lines - 1, line(lax.rem(late, lines)))
+
+    for late in range(pairs - LAG, pairs):
+        if late % lines:
+            join(late // lines, line(late % lines))
+
+    @pl.loop(0, groups)
+    def _(g):
+        for copy in part_y(g, z):
+            copy.wait_recv()
+        for d in range(1, lines):
+            for copy in part_z(g, line(d), line(d)):
+                copy.wait_recv()
+        others = [line(d) for d in range(1, lines)]
+        stats = [fstat[g], stat[g, y, z], ystat[g, z]] + [zstat[g, zz] for zz in others]
+        parts = [facc[g], part[g, y, z], ypart[g, z]] + [zpart[g, zz] for zz in others]
+        top = functools.reduce(jnp.maximum, [s[0:1] for s in stats])
+        factors = [jnp.exp2(s[0:1] - top) for s in stats]
+        total = sum(s[1:2] * f for s, f in zip(stats, factors))
+        factors = columns_of([f / total for f in factors])
+        attention = sum(p.astype(f32) * f for p, f in zip(parts, factors))
+        square = jnp.zeros((rows, hd), f32)
+        for j in range(per):
+            at = slice(j * hd, (j + 1) * hd)
+            state = hs[g, :, at] + attention[j * rows : (j + 1) * rows]
+            hs[g, :, at] = state
+            square += state * state
+        sq[2 + g] = square
+
+    square = sum(sq[2 + g] for g in range(groups))
+    sq[0] = jnp.broadcast_to(jnp.sum(square, axis=-1, keepdims=True), (rows, 128))
+    square_copy = remote(sq.at[0], sq.at[1], sq_sem, (0,), (0,), to_core())
+    square_copy.start()
+    square_copy.wait_recv()
+    inverse = lax.rsqrt((sq[0] + sq[1])[:, 0:1] / (2 * width) + EPSILON)
+
+    for g in range(groups):
+        gain = gain_ref[:, g * group_width : (g + 1) * group_width]
+        nbuf[g, y, z] = (hs[g] * inverse * gain).astype(bf16)
+        gather_y(nbuf, ny_sem, g, z).start()
+        for d in range(1, lines):
+            gather_z(nbuf, nz_sem, g, d).start()
+
+    def forward(g):
+        for d in range(1, lines):
+            gather_z_arrival(nbuf, nz_sem, g, line(d)).wait_recv()
+            gather_y(nbuf, ny_sem, g, line(d)).start()
+
+    @pl.loop(0, pairs)
+    def _(p):
+        for copy in gate_up_copies(p):
+            copy.wait()
+
+    all_rows = 2 * lines * rows
+    tiles = 2 * half // TILE
+
+    def swap(t):
+        return remote(gacc.at[0, t], grecv.at[t], g_sem, (t,), (t,), to_core())
+
+    def gate_up(g, slot, at):
+        @pl.loop(0, tiles)
+        def _(t):
+            gacc[slot, t] += jnp.dot(
+                nbuf[g].reshape(all_rows, group_width),
+                wgu[
+                    at,
+                    pl.ds(pl.multiple_of(g * group_width, group_width), group_width),
+                    pl.ds(pl.multiple_of(t * TILE, TILE), TILE),
+                ],
+                preferred_element_type=f32,
+            )
+            if slot == 0:
+
+                @pl.when(g == groups - 1)
+                def _():
+                    swap(t).start()
+
+    forward(0)
+
+    @pl.loop(0, groups)
+    def _(g):
+        @pl.when(g < groups - 1)
+        def _():
+            forward(g + 1)
+
+        for d in range(lines):
+            gather_y_arrival(nbuf, ny_sem, g, line(d)).wait_recv()
+        gate_up(g, 0, 1 - core)
+        gate_up(g, 1, core)
+
+    for t in range(tiles):
+        swap(t).wait_recv()
+    for b in range(half // 128):
+
+        def summed(column):
+            t, at = column // TILE, slice(column % TILE, column % TILE + 128)
+            return gacc[1, t, :, at] + grecv[t, :, at]
+
+        gate, up = summed(b * 128), summed(half + b * 128)
+        hbuf[:, pl.ds(pl.multiple_of(core * half + b * 128, 128), 128)] = (
+            gate / (1.0 + jnp.exp(-gate)) * up
+        ).astype(bf16)
+
+    def hidden_copy(at):
+        both = hbuf.at[:, pl.ds(pl.multiple_of(at * half, 128), half)]
+        return remote(both, both, h_sem, (0,), (0,), to_core())
+
+    hidden_copy(core).start()
+
+    @pl.loop(0, pairs)
+    def _(p):
+        down_copy(p).wait()
+
+    hidden_copy(1 - core).wait_recv()
+
+    chunk = width // CHUNKS
+
+    def down_y(c):
+        return remote(dpart.at[c], dy.at[c], dy_sem, (c,), (c,), to_y())
+
+    def down_z(c, zz, at):
+        return remote(dsum.at[c, zz], dz.at[c, at], dz_sem, (c, zz), (c, at), to_z(zz))
+
+    def relay(c):
+        down_y(c).wait_recv()
+        for d in range(1, lines):
+            zz = line(d)
+            dsum[c, zz] = (dacc[c, y, zz] + dy[c, zz].astype(f32)).astype(bf16)
+            down_z(c, zz, z).start()
+
+    @pl.loop(0, CHUNKS)
+    def _(c):
+        for t in range(chunk // TILE):
+            dacc[c, :, :, :, t * TILE : (t + 1) * TILE] = jnp.dot(
+                hbuf[...],
+                wd[:, pl.ds(pl.multiple_of(c * chunk + t * TILE, TILE), TILE)],
+                preferred_element_type=f32,
+            ).reshape(2, lines, rows, TILE)
+        dpart[c] = dacc[c, 1 - y].astype(bf16)
+        down_y(c).start()
+
+        @pl.when(c >= LAG)
+        def _():
+            relay(c - LAG)
+
+    for c in range(CHUNKS - LAG, CHUNKS):
+        relay(c)
+    for c in range(CHUNKS):
+        g, first = c * chunk // group_width, c * chunk % group_width
+        value = hs[g, :, first : first + chunk] + dacc[c, y, z] + dy[c, z].astype(f32)
+        for d in range(1, lines):
+            down_z(c, line(d), line(d)).wait_recv()
+            value += dz[c, line(d)].astype(f32)
+        out_ref[:, :, c * chunk : (c + 1) * chunk] = value.astype(out_ref.dtype).reshape(
+            local_rows, steps, chunk
+        )
+
+    @pl.loop(0, groups)
+    def _(g):
+        for d in range(1, lines):
+            gather_z(qbuf, qz_sem, g, d).wait_send()
+            gather_z(nbuf, nz_sem, g, d).wait_send()
+            for copy in part_z(g, line(d), z):
+                copy.wait_send()
+        for d in range(lines):
+            gather_y(qbuf, qy_sem, g, line(d)).wait_send()
+            gather_y(nbuf, ny_sem, g, line(d)).wait_send()
+            for copy in part_y(g, line(d)):
+                copy.wait_send()
+
+    @pl.loop(0, CHUNKS)
+    def _(c):
+        down_y(c).wait_send()
+        for d in range(1, lines):
+            down_z(c, line(d), z).wait_send()
+
+    for t in range(tiles):
+        swap(t).wait_send()
+    square_copy.wait_send()
+    hidden_copy(core).wait_send()
+
+
+def kernel_body(
+    lines,
+    queries,
+    fresh_keys,
+    fresh_values,
+    residual_in,
+    cache_keys,
+    cache_values,
+    key_scales,
+    value_scales,
+    page_table,
+    row_lengths,
+    norm_gain,
+    w_gate,
+    w_up,
+    w_down,
+):
+    local_rows, steps, width = queries.shape
+    groups, span, hd = cache_keys.shape
+    rows = local_rows * steps
+    group_width = width // groups
+    stack = rows * group_width // hd
+    fresh_width = fresh_keys.shape[2]
+    hidden = w_gate.shape[1]
+    half = hidden // 2
+    tiles = hidden // TILE
+    chunk = width // CHUNKS
+    all_rows = 2 * lines * rows
+    bf16, f32 = jnp.bfloat16, jnp.float32
+    vmem = pl.BlockSpec(memory_space=pltpu.VMEM)
+    smem = pl.BlockSpec(memory_space=pltpu.SMEM)
+    anywhere = pl.BlockSpec(memory_space=pl.ANY)
+    dma = pltpu.SemaphoreType.DMA
+    return pl.pallas_call(
+        functools.partial(layer_kernel, lines),
+        out_shape=jax.ShapeDtypeStruct(queries.shape, bf16),
+        in_specs=[vmem] * 4 + [smem] + [vmem] * 4 + [anywhere] * 5,
+        out_specs=vmem,
+        scratch_shapes=[
+            pltpu.VMEM((groups, span, hd), bf16),
+            pltpu.VMEM((groups, span, hd), bf16),
+            pltpu.VMEM((2, width, 2 * half), bf16),
+            pltpu.VMEM(w_down.shape, bf16),
+            pltpu.VMEM((groups, 2, lines, rows, group_width), bf16),
+            pltpu.VMEM((2, lines, stack, 1), jnp.int32),
+            pltpu.VMEM((groups, 1, span), f32),
+            pltpu.VMEM((groups, 1, span), f32),
+            pltpu.VMEM((1, span), jnp.int32),
+            pltpu.VMEM((128, fresh_width), bf16),
+            pltpu.VMEM((128, fresh_width), bf16),
+            pltpu.VMEM((groups, stack, hd), f32),
+            pltpu.VMEM((groups, 2, stack), f32),
+            pltpu.VMEM((groups, 2, lines, stack, hd), bf16),
+            pltpu.VMEM((groups, 2, lines, 2, stack), f32),
+            pltpu.VMEM((groups, lines, stack, hd), bf16),
+            pltpu.VMEM((groups, lines, 2, stack), f32),
+            pltpu.VMEM((groups, lines, stack, hd), bf16),
+            pltpu.VMEM((groups, lines, 2, stack), f32),
+            pltpu.VMEM((groups, lines, stack, hd), bf16),
+            pltpu.VMEM((groups, lines, 2, stack), f32),
+            pltpu.VMEM((groups, rows, group_width), f32),
+            pltpu.VMEM((2 + groups, rows, 128), f32),
+            pltpu.VMEM((groups, 2, lines, rows, group_width), bf16),
+            pltpu.VMEM((2, tiles, all_rows, TILE), f32),
+            pltpu.VMEM((tiles, all_rows, TILE), f32),
+            pltpu.VMEM((all_rows, hidden), bf16),
+            pltpu.VMEM((CHUNKS, 2, lines, rows, chunk), f32),
+            pltpu.VMEM((CHUNKS, lines, rows, chunk), bf16),
+            pltpu.VMEM((CHUNKS, lines, rows, chunk), bf16),
+            pltpu.VMEM((CHUNKS, lines, rows, chunk), bf16),
+            pltpu.VMEM((CHUNKS, lines, rows, chunk), bf16),
+            dma((2,)),
+            dma((5, groups * lines)),
+            dma((2, groups, lines)),
+            dma((2, groups, lines)),
+            dma((2, 2, groups, lines)),
+            dma((2, 2, groups, lines)),
+            dma((2, 1)),
+            dma((2, groups, lines)),
+            dma((2, groups, lines)),
+            dma((2, tiles)),
+            dma((2, 1)),
+            dma((2, CHUNKS)),
+            dma((2, CHUNKS, lines)),
+        ],
+        compiler_params=pltpu.CompilerParams(
+            collective_id=0, has_side_effects=True, vmem_limit_bytes=62 * 1024 * 1024
+        ),
+    )(
+        queries,
+        fresh_keys,
+        fresh_values,
+        residual_in,
+        row_lengths,
+        key_scales,
+        value_scales,
+        page_table,
+        norm_gain.reshape(1, width),
+        cache_keys,
+        cache_values,
+        w_gate,
+        w_up,
+        w_down,
+    )
+
+
+def choose_body(seq_size, cores, *args):
+    local_rows, steps, width = args[0].shape
+    groups, _, head_dim = args[4].shape
+    rows, hidden = local_rows * steps, args[11].shape[1]
+    stack = rows * width // (groups * head_dim)
+    pairs = groups * (seq_size // 2)
+    weights = 2 * 3 * width * hidden
+    fits = (
+        cores == 2
+        and seq_size % 2 == 0
+        and pairs > LAG
+        and rows % 16 == 0
+        and stack == 128
+        and head_dim == 128
+        and hidden % 256 == 0
+        and hidden % (16 * pairs) == 0
+        and width % (16 * pairs) == 0
+        and width % (CHUNKS * TILE) == 0
+        and CHUNKS % groups == 0
+        and weights <= 44 * 1024 * 1024
+    )
+    if fits:
+        return kernel_body(seq_size // 2, *args)
+    return plain_body(*args)
+
+
 def solution(mesh):
     in_specs = (
         P(("groups", "seq"), None, "tensor"),
@@ -152,4 +767,5 @@
         P("seq", "tensor"),
     )
     out_specs = P(("groups", "seq"), None, "tensor")
+    body = functools.partial(choose_body, mesh.shape["seq"], mesh.shape["tensor"])
     return jax.shard_map(body, mesh=mesh, in_specs=in_specs, out_specs=out_specs, check_vma=False)

time: 390 us -> 118 us (0.30)
  waiting for transfers between devices: 164 us -> 0 us
  blocking collectives: 134 us -> 0 us
  Pallas kernels: 0 us -> 116 us
  matrix products: 50.9 us -> 0 us
  between operations: 13.3 us -> 0.01 us
  local copies, waits for them, and re-layouts: 14.4 us -> 1.65 us
  other arithmetic: 12.1 us -> 0 us
    pallas_call x0 -> x1, Pallas kernels: none -> 116 us  [kernel_body(): pl.pallas_call(functools.partial(layer_kernel, lines), out_shape=jax.Shap...]
    all_gather x2 -> x0, waiting for transfers between devices: 74.2 us -> none  [the longest x1 42.6 us: body(): lax.all_gather(queries, 'seq', axis=0, tiled=True)]
    reduce_scatter x1 -> x0, waiting for transfers between devices: 69.6 us -> none  [body(): lax.psum_scatter(jnp.dot(hidden, w_down, preferred_element_type=jnp.float...]
    all_gather x2 -> x0, blocking collectives: 62.8 us -> none  [the longest x1 32 us: body(): lax.all_gather(fresh_keys, 'seq', axis=0, tiled=True)]
    dot_general x13 -> x0, matrix products: 50.9 us -> none  [the longest x4 10.1 us: per_group(): jnp.einsum('nsqc,cd->nsqd', weights, value_block, preferred_element_type=...]
    psum x2 -> x0, blocking collectives: 36.7 us -> none  [the longest x1 34.1 us: body(): lax.psum((partial_value[1] * factor, partial_value[2] * factor[..., None]...]
    pmax x1 -> x0, blocking collectives: 34.9 us -> none  [body(): row_peak = lax.pmax(partial_value[0], 'seq')]
    psum x2 -> x0, waiting for transfers between devices: 19.8 us -> none  [the longest x1 19.7 us: body(): gate_sums, up_sums = lax.psum((gate_part, up_part), 'tensor')]
  transfers between devices with their start and end apart: 5 -> 0, of which waited for: 4 -> 0; matrix products, arithmetic and copies ran while one was open for 4% -> 0% of each run, Pallas kernels for 0% -> 0%
where the time goes in v2:
time: 118 us
  Pallas kernels  116 us (98%)
  local copies, waits for them, and re-layouts  1.65 us (1%)
    pallas_call x1, Pallas kernels, kernel_body(): pl.pallas_call(functools.partial(layer_kernel, lines), out_shape=jax.Shap...  116 us

profile of v2, /device:TPU:0, one launch (start us, length us, event | category | flops | bytes accessed | tf_op | source)
XLA Modules:
  0.0 117.7 jit_solution(12836773044560835909)
XLA Ops:
  0.0 116.0 %shard_map.136 = bf16[8,2,4096]{2,1,0:T(2,128)(2,1)} custom-call(bf16[8,2,4096]{2,1,0:T(2,128)(2,1)} %q_ref.1, bf16[8,2,512]{2,1,0:T(2,128)(2,1)} %fk_ref.1, bf16[8,2,512]{2,1,0:T(2,128)(2,1)} %fv_ref.1, bf16[8,2,4096]{2,1,0:T(2,128)(2,1)} %res_ref.1, s32[64]{0:T(128)} %lens_ref.1, f32[4,8]{1,0:T(4,128)} %ks_ref.1, f32[4,8]{1,0:T(4,128)} %vs_ref.1, ...), custom_call_target="tpu_custom_call" | custom-call | tf_op jit(solution)/shard_map/pallas_call | solution.py:653
  116.0 1.7 %copy.16 = bf16[8,2,4096]{2,1,0:T(2,128)(2,1)} copy(bf16[8,2,4096]{2,1,0:T(2,128)(2,1)} %shard_map.136) | data formatting | bytes 262144

commit v3 on v2

--- a/solution.py
+++ b/solution.py
@@ -154,7 +154,7 @@
     ks_ref,
     vs_ref,
     pt_ref,
-    gain_ref,
+    gain,
     ck_hbm,
     cv_hbm,
     wg_hbm,
@@ -184,6 +184,7 @@
     zstat,
     hs,
     sq,
+    ibuf,
     nbuf,
     gacc,
     grecv,
@@ -200,6 +201,8 @@
     py_sem,
     pz_sem,
     sq_sem,
+    iz_sem,
+    iy_sem,
     nz_sem,
     ny_sem,
     g_sem,
@@ -299,15 +302,13 @@
         for d in range(1, lines):
             gather_z(qbuf, qz_sem, g, d).start()
 
+    tall = lines * stack
     row_of = lax.rem(lax.broadcasted_iota(jnp.int32, (stack, 1), 0), rows) // steps
-
-    @pl.loop(0, 2 * lines)
-    def _(k):
-        yy, zz = lax.rem(k, 2), k // 2
+    for k in range(2 * lines):
         value = jnp.zeros((stack, 1), jnp.int32)
         for r in range(local_rows):
             value = jnp.where(row_of == r, lens_ref[k * local_rows + r], value)
-        lens[yy, zz] = value
+        lens[k % 2, k // 2 * stack : (k // 2 + 1) * stack] = value
 
     owner = lax.broadcasted_iota(jnp.int32, (1, span), 1) // page
     within = lax.rem(lax.broadcasted_iota(jnp.int32, (1, span), 1), page)
@@ -324,20 +325,20 @@
         krow[g] = k_line * inv_root
         vrow[g] = v_line
 
-    lane = lax.broadcasted_iota(jnp.int32, (stack, 128), 1)
-    sublane = lax.broadcasted_iota(jnp.int32, (128, stack), 0)
-
     def stacked(block):
-        return jnp.concatenate([block[:, j * hd : (j + 1) * hd] for j in range(per)], axis=0)
+        return [block[:, j * hd : (j + 1) * hd] for j in range(per)]
 
     def softmax_terms(scores):
         top = jnp.maximum(jnp.ceil(jnp.max(scores, axis=-1, keepdims=True)), FLOOR)
         terms = jnp.exp2(scores - top)
         total = jnp.sum(terms, axis=-1, keepdims=True)
+        lane = lax.broadcasted_iota(jnp.int32, (scores.shape[0], 128), 1)
         return terms, jnp.where(lane == 0, top, total).T[0:2]
 
     def columns_of(lines_in):
-        table = jnp.zeros((128, stack), f32)
+        shape = (128, lines_in[0].shape[1])
+        sublane = lax.broadcasted_iota(jnp.int32, shape, 0)
+        table = jnp.zeros(shape, f32)
         for i, value in enumerate(lines_in):
             table = jnp.where(sublane == i, value, table)
         table = table.T
@@ -354,7 +355,7 @@
     for g in range(groups):
         at = slice(g * hd, (g + 1) * hd)
         scores = lax.dot_general(
-            stacked(qbuf.at[g, y, z]),
+            jnp.concatenate(stacked(qbuf.at[g, y, z]), axis=0),
             fkp[:, at],
             (((1,), (1,)), ((), ())),
             preferred_element_type=f32,
@@ -369,87 +370,59 @@
     for copy in cache_copies:
         copy.wait()
 
-    def attend(g, yy, zz):
+    def attend(g, yy):
+        heads = [head for zz in range(lines) for head in stacked(qbuf.at[g, yy, zz])]
         scores = lax.dot_general(
-            stacked(qbuf.at[g, yy, zz]),
+            jnp.concatenate(heads, axis=0),
             kbuf[g],
             (((1,), (1,)), ((), ())),
             preferred_element_type=f32,
         )
-        scores = jnp.where(prow[...] < lens[yy, zz], scores * krow[g], NEG_FILL)
-        terms, stat[g, yy, zz] = softmax_terms(scores)
-        part[g, yy, zz] = jnp.dot(
-            (terms * vrow[g]).astype(bf16), vbuf[g], preferred_element_type=f32
-        ).astype(bf16)
-
-    def part_y(g, zz):
-        src = (part.at[g, 1 - y, zz], stat.at[g, 1 - y, zz])
-        dst = (ypart.at[g, zz], ystat.at[g, zz])
-        return [remote(src[i], dst[i], py_sem, (i, g, zz), (i, g, zz), to_y()) for i in range(2)]
+        scores = jnp.where(prow[...] < lens[yy], scores * krow[g], NEG_FILL)
+        terms, stat[g, yy] = softmax_terms(scores)
+        part[g, yy] = (
+            jnp.dot((terms * vrow[g]).astype(bf16), vbuf[g], preferred_element_type=f32)
+            .astype(bf16)
+            .reshape(lines, stack, hd)
+        )
+
+    def part_y(g):
+        src = (part.at[g, 1 - y], stat.at[g, 1 - y])
+        dst = (ypart.at[g], ystat.at[g])
+        return [remote(src[i], dst[i], py_sem, (i, g), (i, g), to_y()) for i in range(2)]
 
     def part_z(g, zz, at):
         src, dst = (spart.at[g, zz], sstat.at[g, zz]), (zpart.at[g, at], zstat.at[g, at])
         return [remote(src[i], dst[i], pz_sem, (i, g, zz), (i, g, at), to_z(zz)) for i in range(2)]
 
-    def join(g, zz):
-        for copy in part_y(g, zz):
+    def join(g):
+        for copy in part_y(g):
             copy.wait_recv()
-        first, second = stat[g, y, zz], ystat[g, zz]
+        first, second = stat[g, y], ystat[g]
         top = jnp.maximum(first[0:1], second[0:1])
         a, b = jnp.exp2(first[0:1] - top), jnp.exp2(second[0:1] - top)
-        sstat[g, zz, 0:1] = top
-        sstat[g, zz, 1:2] = first[1:2] * a + second[1:2] * b
+        total = first[1:2] * a + second[1:2] * b
+        for zz in range(lines):
+            at = slice(zz * stack, (zz + 1) * stack)
+            sstat[g, zz, 0:1] = top[:, at]
+            sstat[g, zz, 1:2] = total[:, at]
         a, b = columns_of([a, b])
-        spart[g, zz] = (part[g, y, zz].astype(f32) * a + ypart[g, zz].astype(f32) * b).astype(bf16)
-        for copy in part_z(g, zz, z):
-            copy.start()
-
-    @pl.loop(0, 2 * pairs)
-    def _(k):
-        pair, other = k // 2, lax.rem(k, 2)
-        g, d = pair // lines, lax.rem(pair, lines)
-        zz = line(d)
-
-        @pl.when(other == 0)
-        def _():
-            for copy in gate_up_copies(pair) + [down_copy(pair)]:
+        joined = (
+            part[g, y].reshape(tall, hd).astype(f32) * a
+            + ypart[g].reshape(tall, hd).astype(f32) * b
+        )
+        spart[g] = joined.astype(bf16).reshape(lines, stack, hd)
+        for d in range(1, lines):
+            for copy in part_z(g, line(d), z):
                 copy.start()
 
-        @pl.when((other == 0) & (d > 0))
-        def _():
-            gather_z_arrival(qbuf, qz_sem, g, zz).wait_recv()
-            gather_y(qbuf, qy_sem, g, zz).start()
-
-        @pl.when(other == 1)
-        def _():
-            gather_y_arrival(qbuf, qy_sem, g, zz).wait_recv()
-
-        attend(g, lax.rem(y + other, 2), zz)
-
-        @pl.when(other == 1)
-        def _():
-            for copy in part_y(g, zz):
-                copy.start()
-
-        late = pair + lines - LAG
-
-        @pl.when((other == 1) & (late >= lines) & (lax.rem(late, lines) > 0))
-        def _():
-            join(late // lines - 1, line(lax.rem(late, lines)))
-
-    for late in range(pairs - LAG, pairs):
-        if late % lines:
-            join(late // lines, line(late % lines))
-
-    @pl.loop(0, groups)
-    def _(g):
-        for copy in part_y(g, z):
-            copy.wait_recv()
-        for d in range(1, lines):
-            for copy in part_z(g, line(d), line(d)):
+    def finish(g):
+        others = [line(d) for d in range(1, lines)]
+        for zz in others:
+            for copy in part_z(g, zz, zz):
                 copy.wait_recv()
-        others = [line(d) for d in range(1, lines)]
-        stats = [fstat[g], stat[g, y, z], ystat[g, z]] + [zstat[g, zz] for zz in others]
+        mine = pl.ds(pl.multiple_of(z * stack, stack), stack)
+        stats = [fstat[g], stat[g, y, :, mine], ystat[g, :, mine]] + [zstat[g, zz] for zz in others]
         parts = [facc[g], part[g, y, z], ypart[g, z]] + [zpart[g, zz] for zz in others]
         top = functools.reduce(jnp.maximum, [s[0:1] for s in stats])
         factors = [jnp.exp2(s[0:1] - top) for s in stats]
@@ -463,30 +436,21 @@
             hs[g, :, at] = state
             square += state * state
         sq[2 + g] = square
-
-    square = sum(sq[2 + g] for g in range(groups))
-    sq[0] = jnp.broadcast_to(jnp.sum(square, axis=-1, keepdims=True), (rows, 128))
-    square_copy = remote(sq.at[0], sq.at[1], sq_sem, (0,), (0,), to_core())
-    square_copy.start()
-    square_copy.wait_recv()
-    inverse = lax.rsqrt((sq[0] + sq[1])[:, 0:1] / (2 * width) + EPSILON)
-
-    for g in range(groups):
-        gain = gain_ref[:, g * group_width : (g + 1) * group_width]
-        nbuf[g, y, z] = (hs[g] * inverse * gain).astype(bf16)
+        nbuf[g, y, z] = (hs[g] * gain[g]).astype(bf16)
         gather_y(nbuf, ny_sem, g, z).start()
         for d in range(1, lines):
             gather_z(nbuf, nz_sem, g, d).start()
 
-    def forward(g):
+    def forward(buf, z_sems, y_sems, g):
         for d in range(1, lines):
-            gather_z_arrival(nbuf, nz_sem, g, line(d)).wait_recv()
-            gather_y(nbuf, ny_sem, g, line(d)).start()
-
-    @pl.loop(0, pairs)
-    def _(p):
-        for copy in gate_up_copies(p):
-            copy.wait()
+            gather_z_arrival(buf, z_sems, g, line(d)).wait_recv()
+            gather_y(buf, y_sems, g, line(d)).start()
+
+    def arrivals(buf, y_sems, g):
+        for d in range(lines):
+            gather_y_arrival(buf, y_sems, g, line(d)).wait_recv()
+
+    square_copy = remote(sq.at[0], sq.at[1], sq_sem, (0,), (0,), to_core())
 
     all_rows = 2 * lines * rows
     tiles = 2 * half // TILE
@@ -494,44 +458,100 @@
     def swap(t):
         return remote(gacc.at[0, t], grecv.at[t], g_sem, (t,), (t,), to_core())
 
-    def gate_up(g, slot, at):
-        @pl.loop(0, tiles)
-        def _(t):
-            gacc[slot, t] += jnp.dot(
-                nbuf[g].reshape(all_rows, group_width),
-                wgu[
-                    at,
-                    pl.ds(pl.multiple_of(g * group_width, group_width), group_width),
-                    pl.ds(pl.multiple_of(t * TILE, TILE), TILE),
-                ],
-                preferred_element_type=f32,
-            )
+    def gate_up(g):
+        for slot, at in ((0, 1 - core), (1, core)):
+            for t in range(tiles):
+                gacc[slot, t] += jnp.dot(
+                    nbuf[g].reshape(all_rows, group_width),
+                    wgu[
+                        at,
+                        pl.ds(pl.multiple_of(g * group_width, group_width), group_width),
+                        t * TILE : (t + 1) * TILE,
+                    ],
+                    preferred_element_type=f32,
+                )
             if slot == 0:
 
                 @pl.when(g == groups - 1)
                 def _():
-                    swap(t).start()
-
-    forward(0)
-
-    @pl.loop(0, groups)
-    def _(g):
-        @pl.when(g < groups - 1)
-        def _():
-            forward(g + 1)
-
-        for d in range(lines):
-            gather_y_arrival(nbuf, ny_sem, g, line(d)).wait_recv()
-        gate_up(g, 0, 1 - core)
-        gate_up(g, 1, core)
-
+                    for t in range(tiles):
+                        swap(t).start()
+
+    forward(qbuf, qz_sem, qy_sem, 0)
+
+    @pl.loop(0, groups + 4)
+    def _(i):
+        @pl.when(i < groups)
+        def _():
+            for p in range(lines):
+                for copy in gate_up_copies(i * lines + p):
+                    copy.start()
+
+        @pl.when(i >= 4)
+        def _():
+            for p in range(lines):
+                down_copy((i - 4) * lines + p).start()
+
+        @pl.when(i + 1 < groups)
+        def _():
+            forward(qbuf, qz_sem, qy_sem, i + 1)
+
+        @pl.when((i >= 3) & (i < groups + 3))
+        def _():
+            forward(nbuf, nz_sem, ny_sem, i - 3)
+
+        @pl.when(i == groups + 2)
+        def _():
+            square_copy.wait_recv()
+            inverse = lax.rsqrt((sq[0] + sq[1]) / (2 * width) + EPSILON)
+            ibuf[0, y, z] = inverse
+            gather_y(ibuf, iy_sem, 0, z).start()
+            for d in range(1, lines):
+                gather_z(ibuf, iz_sem, 0, d).start()
+
+        @pl.when(i == groups + 3)
+        def _():
+            forward(ibuf, iz_sem, iy_sem, 0)
+
+        @pl.when((i >= 1) & (i < groups + 1))
+        def _():
+            join(i - 1)
+
+        @pl.when((i >= 2) & (i < groups + 2))
+        def _():
+            finish(i - 2)
+
+        @pl.when(i == groups + 1)
+        def _():
+            square = sum(sq[2 + g] for g in range(groups))
+            sq[0] = jnp.broadcast_to(jnp.sum(square, axis=-1, keepdims=True), (rows, 128))
+            square_copy.start()
+
+        @pl.when(i < groups)
+        def _():
+            attend(i, y)
+            arrivals(qbuf, qy_sem, i)
+            attend(i, 1 - y)
+            for copy in part_y(i):
+                copy.start()
+
+        @pl.when(i >= 4)
+        def _():
+            for p in range(lines):
+                for copy in gate_up_copies((i - 4) * lines + p):
+                    copy.wait()
+            arrivals(nbuf, ny_sem, i - 4)
+            gate_up(i - 4)
+
+    arrivals(ibuf, iy_sem, 0)
     for t in range(tiles):
         swap(t).wait_recv()
     for b in range(half // 128):
+        inverse = ibuf[0].reshape(all_rows, 128)
 
         def summed(column):
             t, at = column // TILE, slice(column % TILE, column % TILE + 128)
-            return gacc[1, t, :, at] + grecv[t, :, at]
+            return (gacc[1, t, :, at] + grecv[t, :, at]) * inverse
 
         gate, up = summed(b * 128), summed(half + b * 128)
         hbuf[:, pl.ds(pl.multiple_of(core * half + b * 128, 128), 128)] = (
@@ -602,8 +622,8 @@
         for d in range(lines):
             gather_y(qbuf, qy_sem, g, line(d)).wait_send()
             gather_y(nbuf, ny_sem, g, line(d)).wait_send()
-            for copy in part_y(g, line(d)):
-                copy.wait_send()
+        for copy in part_y(g):
+            copy.wait_send()
 
     @pl.loop(0, CHUNKS)
     def _(c):
@@ -613,6 +633,10 @@
 
     for t in range(tiles):
         swap(t).wait_send()
+    for d in range(1, lines):
+        gather_z(ibuf, iz_sem, 0, d).wait_send()
+    for d in range(lines):
+        gather_y(ibuf, iy_sem, 0, line(d)).wait_send()
     square_copy.wait_send()
     hidden_copy(core).wait_send()
 
@@ -661,7 +685,7 @@
             pltpu.VMEM((2, width, 2 * half), bf16),
             pltpu.VMEM(w_down.shape, bf16),
             pltpu.VMEM((groups, 2, lines, rows, group_width), bf16),
-            pltpu.VMEM((2, lines, stack, 1), jnp.int32),
+            pltpu.VMEM((2, lines * stack, 1), jnp.int32),
             pltpu.VMEM((groups, 1, span), f32),
             pltpu.VMEM((groups, 1, span), f32),
             pltpu.VMEM((1, span), jnp.int32),
@@ -670,15 +694,16 @@
             pltpu.VMEM((groups, stack, hd), f32),
             pltpu.VMEM((groups, 2, stack), f32),
             pltpu.VMEM((groups, 2, lines, stack, hd), bf16),
-            pltpu.VMEM((groups, 2, lines, 2, stack), f32),
+            pltpu.VMEM((groups, 2, 2, lines * stack), f32),
             pltpu.VMEM((groups, lines, stack, hd), bf16),
-            pltpu.VMEM((groups, lines, 2, stack), f32),
+            pltpu.VMEM((groups, 2, lines * stack), f32),
             pltpu.VMEM((groups, lines, stack, hd), bf16),
             pltpu.VMEM((groups, lines, 2, stack), f32),
             pltpu.VMEM((groups, lines, stack, hd), bf16),
             pltpu.VMEM((groups, lines, 2, stack), f32),
             pltpu.VMEM((groups, rows, group_width), f32),
             pltpu.VMEM((2 + groups, rows, 128), f32),
+            pltpu.VMEM((1, 2, lines, rows, 128), f32),
             pltpu.VMEM((groups, 2, lines, rows, group_width), bf16),
             pltpu.VMEM((2, tiles, all_rows, TILE), f32),
             pltpu.VMEM((tiles, all_rows, TILE), f32),
@@ -692,9 +717,11 @@
             dma((5, groups * lines)),
             dma((2, groups, lines)),
             dma((2, groups, lines)),
-            dma((2, 2, groups, lines)),
+            dma((2, 2, groups)),
             dma((2, 2, groups, lines)),
             dma((2, 1)),
+            dma((2, 1, lines)),
+            dma((2, 1, lines)),
             dma((2, groups, lines)),
             dma((2, groups, lines)),
             dma((2, tiles)),
@@ -714,7 +741,7 @@
         key_scales,
         value_scales,
         page_table,
-        norm_gain.reshape(1, width),
+        norm_gain.reshape(groups, 1, group_width),
         cache_keys,
         cache_values,
         w_gate,
@@ -733,7 +760,6 @@
     fits = (
         cores == 2
         and seq_size % 2 == 0
-        and pairs > LAG
         and rows % 16 == 0
         and stack == 128
         and head_dim == 128

time: 118 us -> 87.8 us (0.74)
  Pallas kernels: 116 us -> 85.9 us
    pallas_call x1, Pallas kernels: 116 us -> 85.9 us  [kernel_body(): pl.pallas_call(functools.partial(layer_kernel, lines), out_shape=jax.Shap...]
where the time goes in v3:
time: 87.8 us; the launch traced here: 87.6 us
  Pallas kernels  85.9 us (98%)
  local copies, waits for them, and re-layouts  1.65 us (2%)
    pallas_call x1, Pallas kernels, kernel_body(): pl.pallas_call(functools.partial(layer_kernel, lines), out_shape=jax.Shap...  85.9 us

profile of v3, /device:TPU:0, one launch (start us, length us, event | category | flops | bytes accessed | tf_op | source)
XLA Modules:
  0.0 87.6 jit_solution(17885002215676907182)
XLA Ops:
  0.0 85.9 %shard_map.136 = bf16[8,2,4096]{2,1,0:T(2,128)(2,1)} custom-call(bf16[8,2,4096]{2,1,0:T(2,128)(2,1)} %q_ref.1, bf16[8,2,512]{2,1,0:T(2,128)(2,1)} %fk_ref.1, bf16[8,2,512]{2,1,0:T(2,128)(2,1)} %fv_ref.1, bf16[8,2,4096]{2,1,0:T(2,128)(2,1)} %res_ref.1, s32[64]{0:T(128)} %lens_ref.1, f32[4,8]{1,0:T(4,128)} %ks_ref.1, f32[4,8]{1,0:T(4,128)} %vs_ref.1, ...), custom_call_target="tpu_custom_call" | custom-call | tf_op jit(solution)/shard_map/pallas_call | solution.py:677
  85.9 1.7 %copy.16 = bf16[8,2,4096]{2,1,0:T(2,128)(2,1)} copy(bf16[8,2,4096]{2,1,0:T(2,128)(2,1)} %shard_map.136) | data formatting | bytes 262144

commit v4 on v3

--- a/solution.py
+++ b/solution.py
@@ -492,9 +492,32 @@
             for p in range(lines):
                 down_copy((i - 4) * lines + p).start()
 
+        @pl.when(i == groups + 3)
+        def _():
+            forward(ibuf, iz_sem, iy_sem, 0)
+
+        @pl.when(i < groups)
+        def _():
+            attend(i, y)
+
         @pl.when(i + 1 < groups)
         def _():
             forward(qbuf, qz_sem, qy_sem, i + 1)
+
+        @pl.when(i < groups)
+        def _():
+            arrivals(qbuf, qy_sem, i)
+            attend(i, 1 - y)
+            for copy in part_y(i):
+                copy.start()
+
+        @pl.when(i >= 4)
+        def _():
+            for p in range(lines):
+                for copy in gate_up_copies((i - 4) * lines + p):
+                    copy.wait()
+            arrivals(nbuf, ny_sem, i - 4)
+            gate_up(i - 4)
 
         @pl.when((i >= 3) & (i < groups + 3))
         def _():
@@ -509,10 +532,6 @@
             for d in range(1, lines):
                 gather_z(ibuf, iz_sem, 0, d).start()
 
-        @pl.when(i == groups + 3)
-        def _():
-            forward(ibuf, iz_sem, iy_sem, 0)
-
         @pl.when((i >= 1) & (i < groups + 1))
         def _():
             join(i - 1)
@@ -526,22 +545,6 @@
             square = sum(sq[2 + g] for g in range(groups))
             sq[0] = jnp.broadcast_to(jnp.sum(square, axis=-1, keepdims=True), (rows, 128))
             square_copy.start()
-
-        @pl.when(i < groups)
-        def _():
-            attend(i, y)
-            arrivals(qbuf, qy_sem, i)
-            attend(i, 1 - y)
-            for copy in part_y(i):
-                copy.start()
-
-        @pl.when(i >= 4)
-        def _():
-            for p in range(lines):
-                for copy in gate_up_copies((i - 4) * lines + p):
-                    copy.wait()
-            arrivals(nbuf, ny_sem, i - 4)
-            gate_up(i - 4)
 
     arrivals(ibuf, iy_sem, 0)
     for t in range(tiles):

time: 87.8 us -> 86.9 us (0.990)
  Pallas kernels: 85.9 us -> 85 us
where the time goes in v4:
time: 86.9 us; the launch traced here: 86.7 us
  Pallas kernels  85 us (98%)
  local copies, waits for them, and re-layouts  1.65 us (2%)
    pallas_call x1, Pallas kernels, kernel_body(): pl.pallas_call(functools.partial(layer_kernel, lines), out_shape=jax.Shap...  85 us

profile of v4, /device:TPU:0, one launch (start us, length us, event | category | flops | bytes accessed | tf_op | source)
XLA Modules:
  0.0 86.7 jit_solution(1453592261662729012)
XLA Ops:
  0.0 85.0 %shard_map.136 = bf16[8,2,4096]{2,1,0:T(2,128)(2,1)} custom-call(bf16[8,2,4096]{2,1,0:T(2,128)(2,1)} %q_ref.1, bf16[8,2,512]{2,1,0:T(2,128)(2,1)} %fk_ref.1, bf16[8,2,512]{2,1,0:T(2,128)(2,1)} %fv_ref.1, bf16[8,2,4096]{2,1,0:T(2,128)(2,1)} %res_ref.1, s32[64]{0:T(128)} %lens_ref.1, f32[4,8]{1,0:T(4,128)} %ks_ref.1, f32[4,8]{1,0:T(4,128)} %vs_ref.1, ...), custom_call_target="tpu_custom_call" | custom-call | tf_op jit(solution)/shard_map/pallas_call | solution.py:680
  85.1 1.7 %copy.16 = bf16[8,2,4096]{2,1,0:T(2,128)(2,1)} copy(bf16[8,2,4096]{2,1,0:T(2,128)(2,1)} %shard_map.136) | data formatting | bytes 262144

commit v5 on v4

--- a/solution.py
+++ b/solution.py
@@ -142,6 +142,7 @@
 CHUNKS = 8
 TILE = 256
 LAG = 3
+WIDE = 4
 
 
 def layer_kernel(
@@ -225,7 +226,6 @@
     page = span // pages
     inv_root = LOG2E / math.sqrt(hd)
     half = hbuf.shape[1] // 2
-    pairs = groups * lines
 
     def line(d):
         return lax.rem(z + d, lines)
@@ -255,7 +255,7 @@
     ]
 
     def gate_up_copies(p):
-        piece = width // pairs
+        piece = width // groups
         at = pl.ds(pl.multiple_of(p * piece, 16), piece)
         return [
             pltpu.make_async_copy(
@@ -268,7 +268,7 @@
         ]
 
     def down_copy(p):
-        piece = wd_hbm.shape[0] // pairs
+        piece = wd_hbm.shape[0] // groups
         at = pl.ds(pl.multiple_of(p * piece, 16), piece)
         return pltpu.make_async_copy(wd_hbm.at[at], wd.at[at], w_sem.at[4, p])
 
@@ -460,16 +460,19 @@
 
     def gate_up(g):
         for slot, at in ((0, 1 - core), (1, core)):
-            for t in range(tiles):
-                gacc[slot, t] += jnp.dot(
+            for first in range(0, tiles, WIDE):
+                last = min(first + WIDE, tiles)
+                product = jnp.dot(
                     nbuf[g].reshape(all_rows, group_width),
                     wgu[
                         at,
                         pl.ds(pl.multiple_of(g * group_width, group_width), group_width),
-                        t * TILE : (t + 1) * TILE,
+                        first * TILE : last * TILE,
                     ],
                     preferred_element_type=f32,
                 )
+                for t in range(first, last):
+                    gacc[slot, t] += product[:, (t - first) * TILE : (t - first + 1) * TILE]
             if slot == 0:
 
                 @pl.when(g == groups - 1)
@@ -483,14 +486,12 @@
     def _(i):
         @pl.when(i < groups)
         def _():
-            for p in range(lines):
-                for copy in gate_up_copies(i * lines + p):
-                    copy.start()
+            for copy in gate_up_copies(i):
+                copy.start()
 
         @pl.when(i >= 4)
         def _():
-            for p in range(lines):
-                down_copy((i - 4) * lines + p).start()
+            down_copy(i - 4).start()
 
         @pl.when(i == groups + 3)
         def _():
@@ -513,9 +514,8 @@
 
         @pl.when(i >= 4)
         def _():
-            for p in range(lines):
-                for copy in gate_up_copies((i - 4) * lines + p):
-                    copy.wait()
+            for copy in gate_up_copies(i - 4):
+                copy.wait()
             arrivals(nbuf, ny_sem, i - 4)
             gate_up(i - 4)
 
@@ -567,7 +567,7 @@
 
     hidden_copy(core).start()
 
-    @pl.loop(0, pairs)
+    @pl.loop(0, groups)
     def _(p):
         down_copy(p).wait()
 
@@ -590,12 +590,11 @@
 
     @pl.loop(0, CHUNKS)
     def _(c):
-        for t in range(chunk // TILE):
-            dacc[c, :, :, :, t * TILE : (t + 1) * TILE] = jnp.dot(
-                hbuf[...],
-                wd[:, pl.ds(pl.multiple_of(c * chunk + t * TILE, TILE), TILE)],
-                preferred_element_type=f32,
-            ).reshape(2, lines, rows, TILE)
+        dacc[c] = jnp.dot(
+            hbuf[...],
+            wd[:, pl.ds(pl.multiple_of(c * chunk, TILE), chunk)],
+            preferred_element_type=f32,
+        ).reshape(2, lines, rows, chunk)
         dpart[c] = dacc[c, 1 - y].astype(bf16)
         down_y(c).start()
 
@@ -717,7 +716,7 @@
             pltpu.VMEM((CHUNKS, lines, rows, chunk), bf16),
             pltpu.VMEM((CHUNKS, lines, rows, chunk), bf16),
             dma((2,)),
-            dma((5, groups * lines)),
+            dma((5, groups)),
             dma((2, groups, lines)),
             dma((2, groups, lines)),
             dma((2, 2, groups)),
@@ -758,7 +757,6 @@
     groups, _, head_dim = args[4].shape
     rows, hidden = local_rows * steps, args[11].shape[1]
     stack = rows * width // (groups * head_dim)
-    pairs = groups * (seq_size // 2)
     weights = 2 * 3 * width * hidden
     fits = (
         cores == 2
@@ -767,8 +765,8 @@
         and stack == 128
         and head_dim == 128
         and hidden % 256 == 0
-        and hidden % (16 * pairs) == 0
-        and width % (16 * pairs) == 0
+        and hidden % (16 * groups) == 0
+        and width % (16 * groups) == 0
         and width % (CHUNKS * TILE) == 0
         and CHUNKS % groups == 0
         and weights <= 44 * 1024 * 1024

time: 86.9 us -> 86.4 us (level)
  no operation moved by 1% of the time
where the time goes in v5:
time: 86.4 us; the launch traced here: 86.2 us
  Pallas kernels  84.5 us (98%)
  local copies, waits for them, and re-layouts  1.65 us (2%)
    pallas_call x1, Pallas kernels, kernel_body(): pl.pallas_call(functools.partial(layer_kernel, lines), out_shape=jax.Shap...  84.5 us

profile of v5, /device:TPU:0, one launch (start us, length us, event | category | flops | bytes accessed | tf_op | source)
XLA Modules:
  0.0 86.2 jit_solution(9068803354352812036)
XLA Ops:
  0.0 84.5 %shard_map.136 = bf16[8,2,4096]{2,1,0:T(2,128)(2,1)} custom-call(bf16[8,2,4096]{2,1,0:T(2,128)(2,1)} %q_ref.1, bf16[8,2,512]{2,1,0:T(2,128)(2,1)} %fk_ref.1, bf16[8,2,512]{2,1,0:T(2,128)(2,1)} %fv_ref.1, bf16[8,2,4096]{2,1,0:T(2,128)(2,1)} %res_ref.1, s32[64]{0:T(128)} %lens_ref.1, f32[4,8]{1,0:T(4,128)} %ks_ref.1, f32[4,8]{1,0:T(4,128)} %vs_ref.1, ...), custom_call_target="tpu_custom_call" | custom-call | tf_op jit(solution)/shard_map/pallas_call | solution.py:679
  84.5 1.7 %copy.16 = bf16[8,2,4096]{2,1,0:T(2,128)(2,1)} copy(bf16[8,2,4096]{2,1,0:T(2,128)(2,1)} %shard_map.136) | data formatting | bytes 262144
